TPU v7x, 128 devices: a whole 4x4x4 slice. The times are simulated.
128 devices in a mesh: space: 8 (over y, core), chan: 16 (over z, x).
Axes of the slice: x: 4, y: 4, z: 4, core: 2. Of those that a mesh axis runs over, the one named last changes fastest.
Arguments:
- volume: bfloat16 [4, 64, 64, 64, 128], P(None, 'space', 'chan'), may hold values from -6 to 6
- w_first: bfloat16 [3, 3, 3, 128, 256], P(None, None, None, None, 'chan'), may hold values from -0.109375 to 0.109375
- w_second: bfloat16 [3, 3, 3, 256, 256], P(None, None, None, None, 'chan'), may hold values from -0.078125 to 0.078125
- cotangent: bfloat16 [4, 16, 16, 16, 256], P(None, 'space', None, None, 'chan'), may hold values from -6 to 6
Outputs:
- second_out: bfloat16 [4, 16, 16, 16, 256], P(None, 'space', None, None, 'chan')
- volume_grad: bfloat16 [4, 64, 64, 64, 128], P(None, 'space', 'chan')
- first_grad: float32 [3, 3, 3, 128, 256], P(None, None, None, None, 'chan')
- second_grad: float32 [3, 3, 3, 256, 256], P(None, None, None, None, 'chan')
All inputs are finite; a program needn't handle non-finite values.
Results may differ from a plain program's by a relative error of at most 0.018.
Values may be sent and summed in bfloat16 or wider, within the bound.
A program may use at most 64 MiB of HBM per device.

v0:
```python
import jax
import jax.numpy as jnp
from jax import lax
from jax.sharding import Mesh
from jax.sharding import PartitionSpec as P

CHAN = ("chan_0", "chan_1")


def from_behind(value, axis, steps):
    count = lax.axis_size(axis)
    first, last = (max(0, -steps), min(count, count - steps))
    return lax.ppermute(value, axis, [(source, source + steps) for source in range(first, last)])


def in_order(tiles, dim):
    lengths = list(tiles.shape[1:])
    lengths[dim] *= tiles.shape[0]
    return jnp.moveaxis(tiles, 0, dim).reshape(lengths)


def from_everyone(array, axis):
    peers = lax.axis_size(axis)
    return lax.all_to_all(
        jnp.broadcast_to(array[None], (peers, *array.shape)), axis, 0, 0, tiled=True
    )


def gather_directly(array, axis, dim):
    return in_order(from_everyone(array, axis), dim)


def scatter_axes(array, axes, dim):
    for axis in axes:
        array = lax.psum_scatter(array, axis, scatter_dimension=dim, tiled=True)
    return array


def taken_together(array, axis):
    everything = from_everyone(array, axis)
    return jnp.sum(everything.astype(jnp.float32), axis=0)


def split_up(array, dim, peers):
    lengths = array.shape
    tiles = array.reshape(*lengths[:dim], peers, lengths[dim] // peers, *lengths[dim + 1 :])
    return jnp.moveaxis(tiles, dim, 0)


def summed_on_arrival(array, axis, dim):
    tiles = split_up(array, dim, lax.axis_size(axis))
    arrived = lax.all_to_all(tiles, axis, split_axis=0, concat_axis=0, tiled=True)
    return arrived.astype(jnp.float32).sum(axis=0)


def conv_forward(padded, filters):
    return lax.conv_general_dilated(
        padded,
        filters,
        (2, 2, 2),
        "VALID",
        dimension_numbers=("NDHWC", "DHWIO", "NDHWC"),
        preferred_element_type=jnp.float32,
    )


def filter_grad(padded, grad_cells):
    result = lax.conv_general_dilated(
        padded,
        grad_cells,
        (1, 1, 1),
        "VALID",
        rhs_dilation=(2, 2, 2),
        dimension_numbers=("CDHWN", "IDHWO", "NDHWC"),
        preferred_element_type=jnp.float32,
    )
    return jnp.transpose(result, (1, 2, 3, 0, 4))


def input_grad(grad_cells, filters):
    flipped = filters[::-1, ::-1, ::-1]
    return lax.conv_general_dilated(
        grad_cells,
        flipped,
        (1, 1, 1),
        ((2, 2), (2, 2), (2, 2)),
        lhs_dilation=(2, 2, 2),
        dimension_numbers=("NDHWC", "DHWOI", "NDHWC"),
        preferred_element_type=jnp.float32,
    )


def local(volume, w_first, w_second, cotangent):
    lower_plane = from_behind(volume[:, -1:], "space", 1)
    stacked = jnp.concatenate([lower_plane, volume], axis=1)
    side_row = from_behind(stacked[:, :, -1:], CHAN, 1)
    vol_pad = jnp.pad(
        jnp.concatenate([side_row, stacked], axis=2), ((0, 0), (0, 0), (0, 0), (1, 0), (0, 0))
    )
    first_full = gather_directly(w_first, CHAN, 4)
    pre_first = conv_forward(vol_pad, first_full)
    hidden_act = jnp.where(pre_first > 0, pre_first, 0.3 * pre_first).astype(jnp.bfloat16)
    second_full = lax.all_gather(w_second, CHAN, axis=4, tiled=True)
    grad_cells = lax.all_to_all(cotangent, CHAN, split_axis=2, concat_axis=4, tiled=True)
    act_lower = from_behind(hidden_act[:, -1:], "space", 1)
    act_stack = jnp.concatenate([act_lower, hidden_act], axis=1)
    act_side = from_behind(act_stack[:, :, -1:], CHAN, 1)
    act_pad = jnp.pad(
        jnp.concatenate([act_side, act_stack], axis=2), ((0, 0), (0, 0), (0, 0), (1, 0), (0, 0))
    )
    local_out = conv_forward(act_pad, second_full).astype(jnp.bfloat16)
    second_out = lax.all_to_all(local_out, CHAN, split_axis=4, concat_axis=2, tiled=True)
    second_terms = filter_grad(act_pad, grad_cells)
    second_shares = scatter_axes(second_terms.astype(jnp.bfloat16), CHAN, 4).astype(jnp.float32)
    second_grad = taken_together(second_shares.astype(jnp.bfloat16), "space").astype(jnp.float32)
    back_pad = input_grad(grad_cells, second_full)
    row_terms = from_behind(back_pad[:, :, :1], CHAN, -1)
    folded = back_pad[:, :, 1:]
    folded = folded.at[:, :, -1:].add(row_terms)
    plane_terms = from_behind(folded[:, :1], "space", -1)
    folded = folded[:, 1:]
    folded = folded.at[:, -1:].add(plane_terms)
    act_back = folded[:, :, :, 1:]
    pre_back = (act_back * jnp.where(pre_first > 0, 1.0, 0.3)).astype(jnp.bfloat16)
    first_terms = filter_grad(vol_pad, pre_back)
    first_shares = summed_on_arrival(first_terms.astype(jnp.bfloat16), CHAN, 4)
    first_grad = taken_together(first_shares.astype(jnp.bfloat16), "space").astype(jnp.float32)
    grad_pad = input_grad(pre_back, first_full)
    row_grad = from_behind(grad_pad[:, :, :1].astype(jnp.bfloat16), CHAN, -1).astype(jnp.float32)
    grad_fold = grad_pad[:, :, 1:]
    grad_fold = grad_fold.at[:, :, -1:].add(row_grad)
    plane_grad = from_behind(grad_fold[:, :1].astype(jnp.bfloat16), "space", -1).astype(jnp.float32)
    grad_fold = grad_fold[:, 1:]
    grad_fold = grad_fold.at[:, -1:].add(plane_grad)
    volume_grad = grad_fold[:, :, :, 1:].astype(jnp.bfloat16)
    return (second_out, volume_grad, first_grad, second_grad)


def solution(mesh):
    finer = Mesh(mesh.devices.reshape(mesh.shape["space"], 4, 4), ("space", "chan_0", "chan_1"))
    placed = (
        P(None, "space", CHAN, None, None),
        P(None, None, None, None, CHAN),
        P(None, None, None, None, CHAN),
        P(None, "space", None, None, CHAN),
    )
    return jax.shard_map(
        local,
        mesh=finer,
        in_specs=placed,
        out_specs=(
            P(None, "space", None, None, CHAN),
            P(None, "space", CHAN, None, None),
            P(None, None, None, None, CHAN),
            P(None, None, None, None, CHAN),
        ),
        check_vma=False,
    )
```

profile of v0, /device:TPU:1, one launch (start us, length us, event | category | flops | bytes accessed | tf_op | source)
XLA Modules:
  0.0 322.6 jit_solution(6459076045353048105)
XLA Ops:
  10.4 14.7 %all_to_all.56 = bf16[16,2,1024]{2,1,0:T(2,128)(2,1)S(1)} all-to-all(bf16[16,2,1024]{2,1,0:T(2,128)(2,1)S(1)} %reshape.218), channel_id=1, replica_groups=mesh['space'=8,'chan_0'=4,'chan_1'=4] {'chan_0','chan_1'}, dimensions={0} | all-to-all | bytes 131072 | tf_op jit(solution)/shard_map/all_to_all | solution.py:104
  27.5 4.5 %all-to-all-start = ((bf16[16,3,3,3,128,16]{4,5,3,2,1,0:T(8,128)(2,1)}), bf16[16,3,3,3,128,16]{4,5,3,2,1,0:T(8,128)(2,1)}, u32[]{:S(2)}, u32[]{:S(2)}) async-start(bf16[16,3,3,3,128,16]{4,5,3,2,1,0:T(8,128)(2,1)} %broadcast_in_dim.12), calls=%async_computation | async-start | bytes 3538944 | tf_op jit(solution)/shard_map/all_to_all | solution.py:24
  32.3 5.2 %collective-permute-start = (bf16[4,1,4,64,128]{4,0,3,2,1:T(4,128)(2,1)S(1)}, bf16[4,1,4,64,128]{4,0,3,2,1:T(4,128)(2,1)S(1)}, u32[]{:S(2)}, u32[]{:S(2)}) collective-permute-start(bf16[4,1,4,64,128]{4,0,3,2,1:T(4,128)(2,1)S(1)} %copy.150), channel_id=1, source_target_pairs={{0,16},{16,32},{32,48},{48,64},{64,80},{80,96},{96,112},{1,17},{17... | collective-permute-start | bytes 786440 | tf_op jit(solution)/shard_map/ppermute | solution.py:13
  37.5 3.3 %collective-permute-done = bf16[4,1,4,64,128]{4,0,3,2,1:T(4,128)(2,1)S(1)} collective-permute-done((bf16[4,1,4,64,128]{4,0,3,2,1:T(4,128)(2,1)S(1)}, bf16[4,1,4,64,128]{4,0,3,2,1:T(4,128)(2,1)S(1)}, u32[]{:S(2)}, u32[]{:S(2)}) %collective-permute-start) | collective-permute-done | bytes 262176 | tf_op jit(solution)/shard_map/ppermute | solution.py:13
  40.9 3.7 %constant_dynamic-update-slice_fusion = bf16[4,9,4,64,128]{4,0,3,2,1:T(4,128)(2,1)S(1)} fusion(bf16[4,9,4,64,128]{4,0,3,2,1:T(4,128)(2,1)S(1)} %constant_dynamic-update-slice_fusion.1, bf16[4,8,4,64,128]{4,3,2,1,0:T(8,128)(2,1)} %param.12), kind=kLoop, calls=%fused_computation.57 | loop fusion | bytes 4194304 | tf_op jit(solution)/shard_map/concatenate | solution.py:95
  45.9 3.6 %collective-permute-start.1 = (bf16[4,9,1,64,128]{4,0,3,2,1:T(4,128)(2,1)}, bf16[4,9,1,64,128]{4,0,3,2,1:T(4,128)(2,1)S(1)}, u32[]{:S(2)}, u32[]{:S(2)}) collective-permute-start(bf16[4,9,1,64,128]{4,0,3,2,1:T(4,128)(2,1)} %slice.218), channel_id=1, source_target_pairs={{0,1},{1,2},{2,3},{3,4},{4,5},{5,6},{6,7},{7,8},{8,9},{9,10},{10,1... | collective-permute-start | bytes 1769480 | tf_op jit(solution)/shard_map/ppermute | solution.py:13
  50.7 22.8 %collective-permute-done.1 = bf16[4,9,1,64,128]{4,0,3,2,1:T(4,128)(2,1)S(1)} collective-permute-done((bf16[4,9,1,64,128]{4,0,3,2,1:T(4,128)(2,1)}, bf16[4,9,1,64,128]{4,0,3,2,1:T(4,128)(2,1)S(1)}, u32[]{:S(2)}, u32[]{:S(2)}) %collective-permute-start.1) | collective-permute-done | bytes 589856 | tf_op jit(solution)/shard_map/ppermute | solution.py:13
  82.3 3.5 %all-gather.2.cloned.1.call-done = bf16[3,3,3,256,256]{3,4,2,1,0:T(8,128)(2,1)} async-done(((bf16[3,3,3,256,16]{3,4,2,1,0:T(8,128)(2,1)}), bf16[3,3,3,256,256]{3,4,2,1,0:T(8,128)(2,1)}) %all-gather.2.cloned.1.call-update) | async-done | bytes 3538960 | tf_op jit(solution)/shard_map/all_gather | solution.py:103
  85.9 4.7 %fusion.46 = f32[4,5,3,33,256]{4,0,3,2,1:T(4,128)S(1)} fusion(bf16[4,2,1,16,256]{4,0,3,2,1:T(4,128)(2,1)S(1)} %all_to_all.46, bf16[3,3,3,256,256]{3,4,2,1,0:T(8,128)(2,1)} %all-gather.2.cloned.1.call-done), kind=kOutput, calls=%fused_computation.69 | convolution fusion | flops 452984832 | bytes 5632000 | tf_op jit(solution)/shard_map/conv_general_dilated | solution.py:82
  92.1 2.7 compare_select_fusion
  95.2 3.9 %collective-permute-start.2 = (bf16[4,1,2,32,256]{4,0,3,2,1:T(4,128)(2,1)S(1)}, bf16[4,1,2,32,256]{4,0,3,2,1:T(4,128)(2,1)S(1)}, u32[]{:S(2)}, u32[]{:S(2)}) collective-permute-start(bf16[4,1,2,32,256]{4,0,3,2,1:T(4,128)(2,1)S(1)} %bitcast.106), channel_id=1, source_target_pairs={{0,16},{16,32},{32,48},{48,64},{64,80},{80,96},{96,112},{1,17},{17... | collective-permute-start | bytes 393224 | tf_op jit(solution)/shard_map/ppermute | solution.py:13
  101.2 4.5 %collective-permute-start.3 = (bf16[4,5,1,32,256]{4,0,3,2,1:T(4,128)(2,1)S(1)}, bf16[4,5,1,32,256]{4,0,3,2,1:T(4,128)(2,1)S(1)}, u32[]{:S(2)}, u32[]{:S(2)}) collective-permute-start(bf16[4,5,1,32,256]{4,0,3,2,1:T(4,128)(2,1)S(1)} %pad_maximum_fusion.2), channel_id=1, source_target_pairs={{0,1},{1,2},{2,3},{3,4},{4,5},{5,6},{6,7},{7,8},{8,9},{9,10},{10,1... | collective-permute-start | bytes 983048 | tf_op jit(solution)/shard_map/ppermute | solution.py:13
  110.6 3.6 %collective-permute-start.5 = (f32[4,1,2,33,256]{4,0,3,2,1:T(4,128)}, f32[4,1,2,33,256]{4,0,3,2,1:T(4,128)}, u32[]{:S(2)}, u32[]{:S(2)}) collective-permute-start(f32[4,1,2,33,256]{4,0,3,2,1:T(4,128)} %slice.230), channel_id=1, source_target_pairs={{16,0},{32,16},{48,32},{64,48},{80,64},{96,80},{112,96},{17,1},{33... | collective-permute-start | bytes 811016 | tf_op jit(solution)/shard_map/ppermute | solution.py:13
  114.2 3.1 convolution_convert_fusion
  121.7 5.8 %convolution_convert_fusion.1 = bf16[3,3,3,128,256]{4,3,2,1,0:T(8,128)(2,1)} fusion(bf16[4,4,2,32,256]{4,0,3,2,1:T(4,128)(2,1)S(1)} %fusion.29, bf16[4,9,4,64,128]{4,0,3,2,1:T(4,128)(2,1)S(1)} %copy-done.5, bf16[4,9,1,64,128]{4,0,3,2,1:T(4,128)(2,1)S(1)} %copy-done.14), kind=kOutput, calls=%fused_computation.25 | convolution fusion | flops 1799847936 | bytes 5242880 | tf_op jit(solution)/shard_map/transpose | solution.py:77
  127.6 4.0 %copy.125 = bf16[3,3,3,128,256]{3,4,2,1,0:T(8,128)(2,1)} copy(bf16[3,3,3,128,256]{4,3,2,1,0:T(8,128)(2,1)} %convolution_convert_fusion.1) | data formatting | bytes 3538944 | tf_op jit(solution)/shard_map/convert_element_type | solution.py:126
  131.5 3.0 copy.126
  134.5 7.7 %all-to-all-start.3 = ((bf16[16,3,3,3,128,16]{4,5,3,2,1,0:T(8,128)(2,1)}), bf16[16,3,3,3,128,16]{4,5,3,2,1,0:T(8,128)(2,1)}, u32[]{:S(2)}, u32[]{:S(2)}) async-start(bf16[16,3,3,3,128,16]{4,5,3,2,1,0:T(8,128)(2,1)} %copy.126), calls=%async_computation.3 | async-start | bytes 3538944 | tf_op jit(solution)/shard_map/all_to_all | solution.py:52
  145.9 33.8 %reduce-scatter.3.cloned.1.call-done = bf16[3,3,3,256,64]{3,4,2,1,0:T(8,128)(2,1)} async-done(((bf16[3,3,3,256,256]{3,4,2,1,0:T(8,128)(2,1)}), bf16[3,3,3,256,64]{3,4,2,1,0:T(8,128)(2,1)}) %reduce-scatter.3.cloned.1.call-update) | async-done | bytes 884752 | tf_op jit(solution)/shard_map/reduce_scatter | solution.py:35
  179.8 3.8 %fusion.26 = bf16[2,1,32,3,256]{4,2,3,1,0:T(8,128)(2,1)S(1)} fusion(bf16[3,3,3,256,256]{3,4,2,1,0:T(8,128)(2,1)} %all-gather.2.cloned.1.call-done, bf16[5,3,4,7,2,256]{5,3,2,4,1,0:T(8,128)(2,1)S(1)} %slice.223, bf16[5,3,4,8,6,256]{5,3,2,4,1,0:T(8,128)(2,1)} %copy-done.9, pred[32,3]{0,1:T(4,128)(4,1)S(1)} %copy-done.16), kind=kOutput, calls=%fused_computation.35 | convolution fusion | flops 685473792 | bytes 5541984 | tf_op jit(solution)/shard_map/conv_general_dilated | solution.py:57
  185.6 5.0 %all-to-all-start.1 = ((bf16[16,2,1024]{2,1,0:T(2,128)(2,1)}), bf16[16,2,1024]{2,1,0:T(2,128)(2,1)S(1)}, u32[]{:S(2)}, u32[]{:S(2)}) async-start(bf16[16,2,1024]{2,1,0:T(2,128)(2,1)} %reshape.216), calls=%async_computation.1 | async-start | bytes 131072 | tf_op jit(solution)/shard_map/all_to_all | solution.py:112
  192.7 4.7 %all-to-all-done.1 = bf16[16,2,1024]{2,1,0:T(2,128)(2,1)S(1)} async-done(((bf16[16,2,1024]{2,1,0:T(2,128)(2,1)}), bf16[16,2,1024]{2,1,0:T(2,128)(2,1)S(1)}, u32[]{:S(2)}, u32[]{:S(2)}) %all-to-all-start.1) | async-done | bytes 65568 | tf_op jit(solution)/shard_map/all_to_all | solution.py:112
  198.4 6.8 %all-to-all-start.4 = ((bf16[8,3,3,3,128,16]{4,5,3,2,1,0:T(8,128)(2,1)}), bf16[8,3,3,3,128,16]{4,5,3,2,1,0:T(8,128)(2,1)S(1)}, u32[]{:S(2)}, u32[]{:S(2)}) async-start(bf16[8,3,3,3,128,16]{4,5,3,2,1,0:T(8,128)(2,1)} %broadcast_in_dim.14), calls=%async_computation.4 | async-start | bytes 1769472 | tf_op jit(solution)/shard_map/all_to_all | solution.py:24
  205.2 7.3 %broadcast_select_fusion = f32[9,5,32,10,128]{4,2,3,1,0:T(8,128)S(1)} fusion(pred[32,10]{0,1:T(8,128)(4,1)S(1)} %copy-done.12, bf16[3,3,3,128,256]{3,4,2,1,0:T(8,128)(2,1)S(1)} %bitcast.88, bf16[4,2,4,8,6,256]{5,2,4,3,1,0:T(4,128)(2,1)S(1)} %fusion.32), kind=kOutput, calls=%fused_computation.12 | convolution fusion | flops 2266767360 | bytes 9929024 | tf_op jit(solution)/shard_map/conv_general_dilated | solution.py:82
  212.5 2.9 copy-done
  218.5 2.6 broadcast_in_dim.15
  221.1 4.6 %all-to-all-start.5 = ((bf16[8,3,3,3,256,16]{4,5,3,2,1,0:T(8,128)(2,1)}), bf16[8,3,3,3,256,16]{4,5,3,2,1,0:T(8,128)(2,1)S(1)}, u32[]{:S(2)}, u32[]{:S(2)}) async-start(bf16[8,3,3,3,256,16]{4,5,3,2,1,0:T(8,128)(2,1)} %broadcast_in_dim.15), calls=%async_computation.7 | async-start | bytes 3538944 | tf_op jit(solution)/shard_map/all_to_all | solution.py:24
  225.7 2.7 slice-done.1
  228.3 3.8 %copy.119 = f32[9,4,32,10,128]{4,1,3,2,0:T(4,128)S(1)} copy(f32[9,4,32,10,128]{4,2,3,1,0:T(8,128)S(1)} %slice-done.1) | data formatting | bytes 11796480 | tf_op jit(solution)/shard_map/conv_general_dilated | solution.py:82
  233.8 2.5 slice_bitcast_fusion
  239.1 61.1 %scatter-add.16 = f32[4,9,4,65,128]{4,2,3,0,1:T(4,128)} dynamic-update-slice(f32[4,9,4,65,128]{4,2,3,0,1:T(4,128)} %slice_bitcast_fusion, f32[4,9,1,65,128]{4,2,3,0,1:T(1,128)S(1)} %copy.124, s32[]{:T(128)} %constant.117.clone.1, s32[]{:T(128)} %constant.117.clone.1, s32[]{:T(128)} %constant.119.clone.1, s32[]{:T(128)} %constant.117.clone.1, s32[]{:T(128)} %constant.117.clone.1) | dynamic-update-slice | bytes 2396164 | tf_op jit(solution)/shard_map/scatter-add | solution.py:131
  304.8 2.9 slice.240
  (120 shorter events, 57.6 us)
Async XLA Ops:
  8.0 77.9 %all-gather.2.cloned.1.call-start = ((), (), s32[]{:S(2)}) async-start(), calls=%async_computation.8 | async-start | bytes 3760128 | tf_op jit(solution)/shard_map/all_gather | solution.py:103
  27.5 4.6 %slice-start.2 = ((bf16[4,8,4,64,128]{4,3,2,1,0:T(8,128)(2,1)}), bf16[4,1,4,64,128]{4,3,2,1,0:T(8,128)(2,1)S(1)}, s32[]{:S(2)}) async-start(bf16[4,8,4,64,128]{4,3,2,1,0:T(8,128)(2,1)} %param.12), calls=%async_computation.13 | async-start | bytes 524288 | tf_op jit(solution)/shard_map/slice | solution.py:94
  27.5 52.9 %all-to-all-start = ((bf16[16,3,3,3,128,16]{4,5,3,2,1,0:T(8,128)(2,1)}), bf16[16,3,3,3,128,16]{4,5,3,2,1,0:T(8,128)(2,1)}, u32[]{:S(2)}, u32[]{:S(2)}) async-start(bf16[16,3,3,3,128,16]{4,5,3,2,1,0:T(8,128)(2,1)} %broadcast_in_dim.12), calls=%async_computation | async-start | bytes 3538944 | tf_op jit(solution)/shard_map/all_to_all | solution.py:24
  32.0 147.7 %reduce-scatter.3.cloned.1.call-start = ((), (), s32[]{:S(2)}) async-start(), calls=%async_computation.9 | async-start | bytes 4423680 | tf_op jit(solution)/shard_map/reduce_scatter | solution.py:35
  32.3 8.5 %collective-permute-start = (bf16[4,1,4,64,128]{4,0,3,2,1:T(4,128)(2,1)S(1)}, bf16[4,1,4,64,128]{4,0,3,2,1:T(4,128)(2,1)S(1)}, u32[]{:S(2)}, u32[]{:S(2)}) collective-permute-start(bf16[4,1,4,64,128]{4,0,3,2,1:T(4,128)(2,1)S(1)} %copy.150), channel_id=1, source_target_pairs={{0,16},{16,32},{32,48},{48,64},{64,80},{80,96},{96,112},{1,17},{17... | collective-permute-start | bytes 786440 | tf_op jit(solution)/shard_map/ppermute | solution.py:13
  44.6 28.9 %copy-start.4 = (bf16[4,9,4,64,128]{4,0,3,2,1:T(4,128)(2,1)}, bf16[4,9,4,64,128]{4,0,3,2,1:T(4,128)(2,1)S(1)}, u32[]{:S(2)}) copy-start(bf16[4,9,4,64,128]{4,0,3,2,1:T(4,128)(2,1)S(1)} %constant_dynamic-update-slice_fusion) | copy-start | bytes 7077892
  45.9 27.6 %collective-permute-start.1 = (bf16[4,9,1,64,128]{4,0,3,2,1:T(4,128)(2,1)}, bf16[4,9,1,64,128]{4,0,3,2,1:T(4,128)(2,1)S(1)}, u32[]{:S(2)}, u32[]{:S(2)}) collective-permute-start(bf16[4,9,1,64,128]{4,0,3,2,1:T(4,128)(2,1)} %slice.218), channel_id=1, source_target_pairs={{0,1},{1,2},{2,3},{3,4},{4,5},{5,6},{6,7},{7,8},{8,9},{9,10},{10,1... | collective-permute-start | bytes 1769480 | tf_op jit(solution)/shard_map/ppermute | solution.py:13
  73.5 1.9 copy-start.13
  82.3 9.7 %copy-start.15 = (pred[32,5]{0,1:T(8,128)(4,1)S(1)}, pred[32,5]{0,1:T(8,128)(4,1)}, u32[]{:S(2)}) copy-start(pred[32,5]{0,1:T(8,128)(4,1)} %constant.138) | copy-start | bytes 484
  85.9 6.2 %copy-start.3 = (bf16[9,5,4,8,10,128]{5,3,2,4,1,0:T(8,128)(2,1)S(1)}, bf16[9,5,4,8,10,128]{5,3,2,4,1,0:T(8,128)(2,1)}, u32[]{:S(2)}) copy-start(bf16[9,5,4,8,10,128]{5,3,2,4,1,0:T(8,128)(2,1)} %copy-done.2) | copy-start | bytes 11059204
  90.7 17.8 %collective-permute-start.4 = (f32[4,5,1,33,256]{4,0,3,2,1:T(4,128)S(1)}, f32[4,5,1,33,256]{4,0,3,2,1:T(4,128)S(1)}, u32[]{:S(2)}, u32[]{:S(2)}) collective-permute-start(f32[4,5,1,33,256]{4,0,3,2,1:T(4,128)S(1)} %slice.227), channel_id=1, source_target_pairs={{1,0},{2,1},{3,2},{4,3},{5,4},{6,5},{7,6},{8,7},{9,8},{10,9},{11,1... | collective-permute-start | bytes 2027528 | tf_op jit(solution)/shard_map/ppermute | solution.py:13
  95.2 5.8 %collective-permute-start.2 = (bf16[4,1,2,32,256]{4,0,3,2,1:T(4,128)(2,1)S(1)}, bf16[4,1,2,32,256]{4,0,3,2,1:T(4,128)(2,1)S(1)}, u32[]{:S(2)}, u32[]{:S(2)}) collective-permute-start(bf16[4,1,2,32,256]{4,0,3,2,1:T(4,128)(2,1)S(1)} %bitcast.106), channel_id=1, source_target_pairs={{0,16},{16,32},{32,48},{48,64},{64,80},{80,96},{96,112},{1,17},{17... | collective-permute-start | bytes 393224 | tf_op jit(solution)/shard_map/ppermute | solution.py:13
  101.2 13.0 %collective-permute-start.3 = (bf16[4,5,1,32,256]{4,0,3,2,1:T(4,128)(2,1)S(1)}, bf16[4,5,1,32,256]{4,0,3,2,1:T(4,128)(2,1)S(1)}, u32[]{:S(2)}, u32[]{:S(2)}) collective-permute-start(bf16[4,5,1,32,256]{4,0,3,2,1:T(4,128)(2,1)S(1)} %pad_maximum_fusion.2), channel_id=1, source_target_pairs={{0,1},{1,2},{2,3},{3,4},{4,5},{5,6},{6,7},{7,8},{8,9},{9,10},{10,1... | collective-permute-start | bytes 983048 | tf_op jit(solution)/shard_map/ppermute | solution.py:13
  110.6 9.2 %collective-permute-start.5 = (f32[4,1,2,33,256]{4,0,3,2,1:T(4,128)}, f32[4,1,2,33,256]{4,0,3,2,1:T(4,128)}, u32[]{:S(2)}, u32[]{:S(2)}) collective-permute-start(f32[4,1,2,33,256]{4,0,3,2,1:T(4,128)} %slice.230), channel_id=1, source_target_pairs={{16,0},{32,16},{48,32},{64,48},{80,64},{96,80},{112,96},{17,1},{33... | collective-permute-start | bytes 811016 | tf_op jit(solution)/shard_map/ppermute | solution.py:13
  117.3 3.6 %copy-start.6 = (f32[4,2,4,32,256]{4,1,3,2,0:T(2,128)S(1)}, f32[4,2,4,32,256]{4,1,3,2,0:T(2,128)}, u32[]{:S(2)}) copy-start(f32[4,2,4,32,256]{4,1,3,2,0:T(2,128)} %slice.232) | copy-start | bytes 3145732
  118.8 2.9 copy-start.5
  118.9 2.9 copy-start.14
  121.7 5.8 %copy-start.10 = (bf16[4,4,2,32,256]{4,0,3,2,1:T(4,128)(2,1)}, bf16[4,4,2,32,256]{4,0,3,2,1:T(4,128)(2,1)S(1)}, u32[]{:S(2)}) copy-start(bf16[4,4,2,32,256]{4,0,3,2,1:T(4,128)(2,1)S(1)} %fusion.29) | copy-start | bytes 1572868
  134.5 51.1 %all-to-all-start.3 = ((bf16[16,3,3,3,128,16]{4,5,3,2,1,0:T(8,128)(2,1)}), bf16[16,3,3,3,128,16]{4,5,3,2,1,0:T(8,128)(2,1)}, u32[]{:S(2)}, u32[]{:S(2)}) async-start(bf16[16,3,3,3,128,16]{4,5,3,2,1,0:T(8,128)(2,1)} %copy.126), calls=%async_computation.3 | async-start | bytes 3538944 | tf_op jit(solution)/shard_map/all_to_all | solution.py:52
  142.3 76.3 %reduce-scatter.5.cloned.1.call-start = ((), (), s32[]{:S(2)}) async-start(), calls=%async_computation.10 | async-start | bytes 1105920 | tf_op jit(solution)/shard_map/reduce_scatter | solution.py:35
  144.2 35.6 %copy-start.16 = (pred[32,3]{0,1:T(4,128)(4,1)S(1)}, pred[32,3]{0,1:T(4,128)(4,1)}, u32[]{:S(2)}) copy-start(pred[32,3]{0,1:T(4,128)(4,1)} %constant.137) | copy-start | bytes 292
  179.8 5.5 %copy-start.11 = (bf16[4,4,2,32,256]{4,0,3,2,1:T(4,128)(2,1)S(1)}, bf16[4,4,2,32,256]{4,0,3,2,1:T(4,128)(2,1)}, u32[]{:S(2)}) copy-start(bf16[4,4,2,32,256]{4,0,3,2,1:T(4,128)(2,1)} %copy-done.10) | copy-start | bytes 1572868
  185.6 11.8 %all-to-all-start.1 = ((bf16[16,2,1024]{2,1,0:T(2,128)(2,1)}), bf16[16,2,1024]{2,1,0:T(2,128)(2,1)S(1)}, u32[]{:S(2)}, u32[]{:S(2)}) async-start(bf16[16,2,1024]{2,1,0:T(2,128)(2,1)} %reshape.216), calls=%async_computation.1 | async-start | bytes 131072 | tf_op jit(solution)/shard_map/all_to_all | solution.py:112
  191.0 14.2 %copy-start.12 = (pred[32,10]{0,1:T(8,128)(4,1)S(1)}, pred[32,10]{0,1:T(8,128)(4,1)}, u32[]{:S(2)}) copy-start(pred[32,10]{0,1:T(8,128)(4,1)} %constant.139) | copy-start | bytes 964
  198.4 20.1 %all-to-all-start.4 = ((bf16[8,3,3,3,128,16]{4,5,3,2,1,0:T(8,128)(2,1)}), bf16[8,3,3,3,128,16]{4,5,3,2,1,0:T(8,128)(2,1)S(1)}, u32[]{:S(2)}, u32[]{:S(2)}) async-start(bf16[8,3,3,3,128,16]{4,5,3,2,1,0:T(8,128)(2,1)} %broadcast_in_dim.14), calls=%async_computation.4 | async-start | bytes 1769472 | tf_op jit(solution)/shard_map/all_to_all | solution.py:24
  212.5 2.9 copy-start
  216.5 19.9 %collective-permute-start.6 = (bf16[4,9,1,65,128]{4,0,3,2,1:T(4,128)(2,1)S(1)}, bf16[4,9,1,65,128]{4,0,3,2,1:T(4,128)(2,1)}, u32[]{:S(2)}, u32[]{:S(2)}) collective-permute-start(bf16[4,9,1,65,128]{4,0,3,2,1:T(4,128)(2,1)S(1)} %copy.123), channel_id=1, source_target_pairs={{1,0},{2,1},{3,2},{4,3},{5,4},{6,5},{7,6},{8,7},{9,8},{10,9},{11,1... | collective-permute-start | bytes 1797128 | tf_op jit(solution)/shard_map/ppermute | solution.py:13
  218.5 2.6 copy-start.7
  221.1 92.9 %all-to-all-start.5 = ((bf16[8,3,3,3,256,16]{4,5,3,2,1,0:T(8,128)(2,1)}), bf16[8,3,3,3,256,16]{4,5,3,2,1,0:T(8,128)(2,1)S(1)}, u32[]{:S(2)}, u32[]{:S(2)}) async-start(bf16[8,3,3,3,256,16]{4,5,3,2,1,0:T(8,128)(2,1)} %broadcast_in_dim.15), calls=%async_computation.7 | async-start | bytes 3538944 | tf_op jit(solution)/shard_map/all_to_all | solution.py:24
  225.7 2.7 slice-start.1
  228.3 3.8 %slice-start = ((f32[9,5,32,10,128]{4,2,3,1,0:T(8,128)}), f32[9,1,32,10,128]{4,2,3,1,0:T(8,128)S(1)}, s32[]{:S(2)}) async-start(f32[9,5,32,10,128]{4,2,3,1,0:T(8,128)} %copy-done), calls=%async_computation.11 | async-start | bytes 2949120 | tf_op jit(solution)/shard_map/conv_general_dilated | solution.py:82
  301.3 7.7 %collective-permute-start.7 = (bf16[4,1,4,65,128]{4,2,3,0,1:T(4,128)(2,1)S(1)}, bf16[4,1,4,65,128]{4,2,3,0,1:T(4,128)(2,1)S(1)}, u32[]{:S(2)}, u32[]{:S(2)}) collective-permute-start(bf16[4,1,4,65,128]{4,2,3,0,1:T(4,128)(2,1)S(1)} %slice.264), channel_id=1, source_target_pairs={{16,0},{32,16},{48,32},{64,48},{80,64},{96,80},{112,96},{17,1},{33... | collective-permute-start | bytes 798728 | tf_op jit(solution)/shard_map/ppermute | solution.py:13
  (4 other events, 5.9 us)
Sparse Core Ops, SparseCore 0:
  10.9 74.8 all-gather.1
Sparse Core Ops, SparseCore 1:
  117.4 62.3 reduce-scatter.2
  182.0 20.9 reduce-scatter.4
where the time goes:
time: 329 us; the launch traced here: 323 us
  local copies, waits for them, and re-layouts  126 us (38%)
  waiting for transfers between devices  72.2 us (22%)
  starting transfers between devices  54.4 us (17%)
  matrix products  27.4 us (8%)
  between operations  16.4 us (5%)
  blocking collectives  14.7 us (4%)
  other arithmetic  11.6 us (4%)
    scatter-add x1, local copies, waits for them, and re-layouts, local(): grad_fold = grad_fold.at[:, :, -1:].add(row_grad)  61.1 us
    reduce_scatter x2, waiting for transfers between devices, scatter_axes(): array = lax.psum_scatter(array, axis, scatter_dimension=dim, tiled=True)  33.8 us
    ppermute x8, waiting for transfers between devices, from_behind(): lax.ppermute(value, axis, [(source, source + steps) for source in range(f...  28.8 us
    ppermute x8, starting transfers between devices, from_behind(): lax.ppermute(value, axis, [(source, source + steps) for source in range(f...  25.3 us
    all_to_all x3, starting transfers between devices, from_everyone(): lax.all_to_all(jnp.broadcast_to(array[None], (peers, *array.shape)), axis...  15.9 us
    all_to_all x1, blocking collectives, local(): lax.all_to_all(cotangent, CHAN, split_axis=2, concat_axis=4, tiled=True)  14.7 us
    unnamed x44, local copies, waits for them, and re-layouts  13.2 us
    conv_general_dilated x2, matrix products, input_grad(): lax.conv_general_dilated(grad_cells, flipped, (1, 1, 1), ((2, 2), (2, 2),...  12 us
  transfers between devices with their start and end apart: 16, of which 10 were waited for; matrix products, arithmetic and copies ran while one was open for 46% of the time, Pallas kernels for 0%

commit v1 on v0

v1 whole, which is shorter than its diff:
```python
import jax
import jax.numpy as jnp
from jax import lax
from jax.experimental import pallas as pl
from jax.experimental.pallas import tpu as pltpu
from jax.sharding import Mesh
from jax.sharding import PartitionSpec as P

MESH = pl.DeviceIdType.MESH
BF = jnp.bfloat16
F32 = jnp.float32
NSEM = 128

SLOT = {}
for _g in range(9):
    _base = 2 * _g if _g < 5 else 14 + 2 * (_g - 5)
    SLOT[3 * _g + 1], SLOT[3 * _g + 2] = _base, _base + 1
    SLOT[3 * _g] = 10 + _g if _g < 4 else 22 + (_g - 4)


def slot(tap):
    return divmod(SLOT[tap], 14)


def uses(cell, count):
    return [(o, cell - 2 * o) for o in range(count) if 0 <= cell - 2 * o <= 2]


PARITY = (((1, 0),), ((0, 1), (2, 0)))


def dot(a, b):
    return lax.dot_general(a, b, (((1,), (0,)), ((), ())), preferred_element_type=F32)


def dot_nt(a, b):
    return lax.dot_general(a, b, (((1,), (1,)), ((), ())), preferred_element_type=F32)


def loop(count, body):
    def step(i, carry):
        body(i)
        return carry

    lax.fori_loop(0, count, step, 0)


def kernel(
    vol, w1, w2, cotl, so, vg, g1, g2,
    xv, im1, im2, wf1, wf2, w1o, w2o, pre, ab, hid, pb0, pb1, pbt, cott, cot0, cot1, fa, fb, vs,
    g1o, g1s, g1r, c1, r1a, r1b, s1a, s1b, q1a, q1b, t1, y1, f1,
    g2o, g2s, g2r, c2, r2a, r2b, s2a, s2b, q2a, q2b, t2, y2, f2,
    ot, sor, ssem, rsem, lsem,
):
    y, core = lax.axis_index("y"), lax.axis_index("core")
    z, x = lax.axis_index("z"), lax.axis_index("x")
    chan = z * 4 + x
    space = y * 2 + core
    sib = {"core": 1 - core}

    def along(name, me, off):
        return {name: lax.rem(me + off, 4)}

    def chan_at(off):
        c = lax.rem(chan + off, 16)
        return {"z": lax.div(c, 4), "x": lax.rem(c, 4)}

    def space_at(off):
        s = lax.rem(space + off, 8)
        return {"y": lax.div(s, 2), "core": lax.rem(s, 2)}

    sent = []

    def put(src, dst, dev):
        n = len(sent)
        copy = pltpu.make_async_remote_copy(
            src_ref=src, dst_ref=dst, send_sem=ssem.at[n], recv_sem=rsem.at[n],
            device_id=dev, device_id_type=MESH,
        )
        copy.start()
        sent.append(copy)
        return copy

    def arrived(copies):
        for copy in copies:
            copy.wait_recv()

    local = pltpu.make_async_copy(vol, xv.at[:, 1:9, 1:5], lsem.at[0])
    local.start()

    for tap in range(27):
        h, l = slot(tap)
        w1o[h, :, l * 128 : (l + 1) * 128] = w1[tap]
        w2o[h, :, l * 256 : (l + 1) * 256] = w2[tap]
    w1o[1, :, 13 * 128 :] = jnp.zeros((16, 128), BF)
    w2o[1, :, 13 * 256 :] = jnp.zeros((16, 256), BF)
    wf1[core, z, x] = w1o[core]
    wf2[core, z, x] = w2o[core]

    barrier = pltpu.get_barrier_semaphore()
    partners = [chan_at(o) for o in range(1, 16)]
    partners += [along("y", y, o) for o in range(1, 4)]
    partners += [sib, {"y": lax.rem(y + 3 + 2 * core, 4), "core": 1 - core}]
    partners += [{**space_at(1), **chan_at(1)}, {**space_at(7), **chan_at(15)}]
    for dev in partners:
        pl.semaphore_signal(barrier, inc=1, device_id=dev, device_id_type=MESH)
    pl.semaphore_wait(barrier, len(partners))

    def spread_first(own, full, q):
        a = [put(own.at[core, :, pl.ds(0, q)], full.at[core, z, x, :, pl.ds(0, q)], along("x", x, o)) for o in (1, 2, 3)]
        b = [put(own.at[core, :, pl.ds(q, q)], full.at[core, z, x, :, pl.ds(q, q)], along("z", z, o)) for o in (1, 2, 3)]
        return a, b

    def spread_second(full, q, first):
        arrived(first[0])
        part = full.at[core, z, :, :, pl.ds(0, q)]
        a = [put(part, part, along("z", z, o)) for o in (1, 2, 3)]
        arrived(first[1])
        part = full.at[core, :, x, :, pl.ds(q, q)]
        b = [put(part, part, along("x", x, o)) for o in (1, 2, 3)]
        return a, b

    def spread_third(full, second):
        arrived(second[0])
        arrived(second[1])
        return put(full.at[core], full.at[core], sib)

    w1_first = spread_first(w1o, wf1, 896)
    vol_halo = [
        put(vol.at[:, :, 3], xv.at[:, 1:9, 0], chan_at(1)),
        put(vol.at[:, 7], xv.at[:, 0, 1:5], space_at(1)),
        put(vol.at[:, 7, 3], xv.at[:, 0, 0], {**space_at(1), **chan_at(1)}),
    ]
    w2_first = spread_first(w2o, wf2, 1792)
    cots = []
    for o in range(1, 16):
        dev = chan_at(o)
        row = dev["z"] * 4 + dev["x"]
        cots.append(put(cotl.at[pl.ds(row, 2)], cott.at[:, chan], dev))
    cott[:, chan] = cotl[pl.ds(chan, 2)]

    fa[:, 0:8, :] = jnp.zeros((5, 8, 128), F32)
    fb[:, 0:8, :] = jnp.zeros((5, 8, 256), F32)

    def patches(blocks):
        def body(v):
            for a, b in blocks:
                fa[b, 8:72, :] = xv[v, a, b].astype(F32)
                parts = [fa[b, pl.ds(7 + k, 32, 2), :].astype(BF) for k in range(3)]
                for p, i in uses(a, 4):
                    for q, j in uses(b, 2):
                        for k in range(3):
                            h, l = slot(9 * i + 3 * j + k)
                            im1[h, q, p, v, :, l * 128 : (l + 1) * 128] = parts[k]

        loop(4, body)

    def blank(v):
        for q in range(2):
            for p in range(4):
                im1[1, q, p, v, :, 13 * 128 :] = jnp.zeros((32, 128), BF)

    loop(4, blank)
    im2[1, :, :, :, 13 * 256 :] = jnp.zeros((2, 4, 16, 256), BF)
    local.wait()
    patches([(a, b) for a in range(1, 9) for b in range(1, 5)])

    w1_second = spread_second(wf1, 896, w1_first)
    w2_second = spread_second(wf2, 1792, w2_first)

    arrived(cots)
    last = lax.broadcasted_iota(jnp.int32, (64, 256), 0) % 16 == 15
    for b in range(2):
        rows = cott[b].reshape(256, 128).astype(F32).T.astype(BF)
        cot0[b, 0:2] = rows.reshape(2, 4, 16, 256)
    cot_halo = put(cot0.at[:, 0], cot0.at[:, 2], space_at(7))

    arrived(vol_halo)

    @pl.when(chan == 0)
    def _():
        xv[:, :, 0] = jnp.zeros((4, 9, 64, 128), BF)

    @pl.when(space == 0)
    def _():
        xv[:, 0] = jnp.zeros((4, 5, 64, 128), BF)

    patches([(a, 0) for a in range(9)] + [(0, b) for b in range(1, 5)])

    w1_third = spread_third(wf1, w1_second)
    arrived([w1_third])

    def conv_first(q):
        def body(n):
            total = jnp.zeros((256, 256), F32)
            for h in range(2):
                total += dot_nt(im1[h, q, pl.ds(2 * n, 2)].reshape(256, 1792), wf1[h].reshape(256, 1792))
            pre[q, pl.ds(2 * n, 2)] = total.reshape(2, 4, 32, 256)
            act = jnp.where(total > 0, total, 0.3 * total).astype(BF)
            hid[q + 1, pl.ds(2 * n + 1, 2)] = act.reshape(2, 4, 32, 256)

        loop(2, body)

    conv_first(1)
    hid_halo = [
        put(hid.at[2, 1:5], hid.at[0, 1:5], chan_at(1)),
        put(hid.at[2, 4], hid.at[0, 0], {**space_at(1), **chan_at(1)}),
    ]
    w2_third = spread_third(wf2, w2_second)
    conv_first(0)
    hid_halo.append(put(hid.at[1:3, 4], hid.at[1:3, 0], space_at(1)))

    arrived([cot_halo])

    @pl.when(space == 7)
    def _():
        cot0[:, 2] = jnp.zeros((2, 4, 16, 256), BF)

    for b in range(2):
        for a in range(3):
            rows = cot0[b, a].reshape(64, 256).astype(F32)
            rows = jnp.where(last, 0.0, pltpu.roll(rows, 63, 0))
            cot1[b, a] = rows.astype(BF).reshape(4, 16, 256)

    arrived([w2_third])

    cot_at = (cot0, cot1)
    for s1 in range(2):
        for s2 in range(2):
            for s3 in range(2):
                total = jnp.zeros((128, 256), F32)
                for i, d1 in PARITY[s1]:
                    for j, d2 in PARITY[s2]:
                        for k, d3 in PARITY[s3]:
                            h, l = slot(9 * i + 3 * j + k)
                            total += dot(
                                cot_at[d3][d2, d1 : d1 + 2].reshape(128, 256),
                                wf2[h, :, :, :, l * 256 : (l + 1) * 256].reshape(256, 256),
                            )
                for a in range(2):
                    for v in range(4):
                        n = (a * 4 + v) * 16
                        for t in range(2):
                            ab[s2, 2 * a + s1, v, t, pl.ds(s3, 16, 2), :] = total[n : n + 16, t * 128 : (t + 1) * 128]

    def back(q):
        for p in range(4):
            slope = jnp.where(pre[q, p] > 0, 1.0, 0.3)
            act_back = jnp.concatenate([ab[q, p, :, 0], ab[q, p, :, 1]], axis=-1)
            rows = act_back * slope
            pb0[q, p] = rows.astype(BF)
            pbt[q, p] = rows.reshape(128, 256).T.astype(BF)

    loop(2, back)
    pb_halo = [
        put(pb0.at[0, 0:4], pb0.at[2, 0:4], chan_at(15)),
        put(pb0.at[0:2, 0], pb0.at[0:2, 4], space_at(7)),
        put(pb0.at[0, 0], pb0.at[2, 4], {**space_at(7), **chan_at(15)}),
    ]

    def first_filters(half, dst, kind):
        lhs = jnp.concatenate([pbt[q, p] for q in range(2) for p in range(4)], axis=1)

        def body(n):
            at = pl.ds(pl.multiple_of(n * 256, 256), 256)
            dst[:, at] = dot(lhs, im1[half, :, :, :, :, at].reshape(1024, 256)).astype(kind)

        loop(7, body)

    first_filters(1 - core, g1s, BF)
    g1_pair = put(g1s, g1r, sib)
    first_filters(core, g1o, F32)

    arrived(hid_halo)

    @pl.when(chan == 0)
    def _():
        hid[0] = jnp.zeros((5, 4, 32, 256), BF)

    @pl.when(space == 0)
    def _():
        hid[:, 0] = jnp.zeros((3, 4, 32, 256), BF)

    def hidden_patches(v):
        for p in range(5):
            for j in range(3):
                fill = hid[j, p, v].astype(F32)
                parts = []
                for t in range(2):
                    fa[p, 8:40, :] = fill[:, t * 128 : (t + 1) * 128]
                    parts.append([fa[p, pl.ds(7 + k, 16, 2), :].astype(BF) for k in range(3)])
                for a, i in uses(p, 2):
                    for k in range(3):
                        h, l = slot(9 * i + 3 * j + k)
                        for t in range(2):
                            im2[h, a, v, :, l * 256 + t * 128 : l * 256 + (t + 1) * 128] = parts[t][k]

    loop(4, hidden_patches)

    def second_filters(half, dst, kind):
        lhs = cott[0].reshape(256, 128)

        def body(n):
            at = pl.ds(pl.multiple_of(n * 512, 512), 512)
            dst[:, at] = dot(lhs, im2[half, :, :, :, at].reshape(128, 512)).astype(kind)

        loop(7, body)

    second_filters(1 - core, g2s, BF)
    g2_pair = put(g2s, g2r, sib)
    second_filters(core, g2o, F32)

    def sum_pair(pair, own, other, chip, q):
        arrived([pair])

        def body(n):
            at = pl.ds(pl.multiple_of(n * 16, 16), 16)
            total = own[at] + other[at].astype(F32)
            chip[lax.div(n, 4), lax.rem(n, 4)] = total.astype(BF)

        loop(16, body)

    def sum_first(chip, ra, rb, q):
        a, b = [], []
        for o in (1, 2, 3):
            to = lax.rem(z + o, 4)
            a.append(put(chip.at[to, :, :, pl.ds(0, q)], ra.at[o - 1], {"z": to}))
            to = lax.rem(x + o, 4)
            b.append(put(chip.at[:, to, :, pl.ds(q, q)], rb.at[o - 1], {"x": to}))
        return a, b

    def sum_second(chip, ra, rb, sa, sb, qa, qb, q, first):
        arrived(first[0])
        total = chip[z, :, :, 0:q].astype(F32)
        for o in range(3):
            total += ra[o].astype(F32)
        sa[...] = total.astype(BF)
        a, b = [], []
        for o in (1, 2, 3):
            to = lax.rem(x + o, 4)
            a.append(put(sa.at[to], qa.at[o - 1], {"x": to}))
        arrived(first[1])
        total = chip[:, x, :, q : 2 * q].astype(F32)
        for o in range(3):
            total += rb[o].astype(F32)
        sb[...] = total.astype(BF)
        for o in (1, 2, 3):
            to = lax.rem(z + o, 4)
            b.append(put(sb.at[to], qb.at[o - 1], {"z": to}))
        return a, b

    def sum_third(sa, sb, qa, qb, t, yr, q, second):
        arrived(second[0])
        total = sa[x].astype(F32)
        for o in range(3):
            total += qa[o].astype(F32)
        t[:, 0:q] = total.astype(BF)
        arrived(second[1])
        total = sb[z].astype(F32)
        for o in range(3):
            total += qb[o].astype(F32)
        t[:, q : 2 * q] = total.astype(BF)
        return [put(t, yr.at[o - 1], along("y", y, o)) for o in (1, 2, 3)]

    def sum_last(t, yr, f, third):
        arrived(third)
        total = t[...].astype(F32)
        for o in range(3):
            total += yr[o].astype(F32)
        f[core] = total
        return put(f.at[core], f.at[core], sib)

    sum_pair(g1_pair, g1o, g1r, c1, 896)
    g1_first = sum_first(c1, r1a, r1b, 896)

    total = jnp.zeros((256, 128), F32)
    for h in range(2):
        total += dot_nt(wf2[h].reshape(256, 3584), im2[h].reshape(128, 3584))
    ot[...] = total.astype(BF).reshape(16, 16, 128)
    outs = []
    for o in range(1, 16):
        dev = chan_at(o)
        outs.append(put(ot.at[dev["z"] * 4 + dev["x"]], sor.at[chan], dev))
    sor[chan] = ot[chan]

    sum_pair(g2_pair, g2o, g2r, c2, 1792)
    g2_first = sum_first(c2, r2a, r2b, 1792)

    arrived(pb_halo)

    @pl.when(chan == 15)
    def _():
        pb0[2] = jnp.zeros((5, 4, 32, 256), BF)

    @pl.when(space == 7)
    def _():
        pb0[:, 4] = jnp.zeros((3, 4, 32, 256), BF)

    edge = lax.broadcasted_iota(jnp.int32, (128, 256), 0) % 32 == 31

    def shifted(q):
        for p in range(5):
            rows = pb0[q, p].reshape(128, 256).astype(F32)
            rows = jnp.where(edge, 0.0, pltpu.roll(rows, 127, 0))
            pb1[q, p] = rows.astype(BF).reshape(4, 32, 256)

    loop(3, shifted)
    g1_second = sum_second(c1, r1a, r1b, s1a, s1b, q1a, q1b, 896, g1_first)

    def volume_grad(q):
        def body(n):
            for s1 in range(2):
                for s2 in range(2):
                    total = jnp.zeros((256, 256), F32)
                    extra = jnp.zeros((256, 128), F32)
                    for i, d1 in PARITY[s1]:
                        for j, d2 in PARITY[s2]:
                            h, l = slot(9 * i + 3 * j + 1)
                            total += dot(
                                pb0[q + d2, pl.ds(2 * n + d1, 2)].reshape(256, 256),
                                wf1[h, :, :, :, l * 128 : (l + 2) * 128].reshape(256, 256),
                            )
                            h, l = slot(9 * i + 3 * j)
                            extra += dot(
                                pb1[q + d2, pl.ds(2 * n + d1, 2)].reshape(256, 256),
                                wf1[h, :, :, :, l * 128 : (l + 1) * 128].reshape(256, 128),
                            )
                    extra += total[:, 128:]
                    for p in range(2):
                        for v in range(4):
                            m = (p * 4 + v) * 32
                            vs[p * 4 + v, pl.ds(0, 32, 2), :] = total[m : m + 32, 0:128]
                            vs[p * 4 + v, pl.ds(1, 32, 2), :] = extra[m : m + 32]
                            vg[v, 4 * n + 2 * p + s1, 2 * q + s2] = vs[p * 4 + v].astype(BF)

        loop(2, body)

    volume_grad(0)
    g1_third = sum_third(s1a, s1b, q1a, q1b, t1, y1, 896, g1_second)
    g2_second = sum_second(c2, r2a, r2b, s2a, s2b, q2a, q2b, 1792, g2_first)
    volume_grad(1)
    g1_last = sum_last(t1, y1, f1, g1_third)
    g2_third = sum_third(s2a, s2b, q2a, q2b, t2, y2, 1792, g2_second)
    arrived(outs)
    so[...] = sor[...]
    arrived([g1_last])
    for tap in range(27):
        h, l = slot(tap)
        g1[tap] = f1[h, :, l * 128 : (l + 1) * 128]
    g2_last = sum_last(t2, y2, f2, g2_third)
    arrived([g2_last])
    for tap in range(27):
        h, l = slot(tap)
        g2[tap] = f2[h, :, l * 256 : (l + 1) * 256]
    for copy in sent:
        copy.wait_send()


def sums(q):
    return [
        pltpu.VMEM((256, 2 * q), F32),
        pltpu.VMEM((256, 2 * q), BF),
        pltpu.VMEM((256, 2 * q), BF),
        pltpu.VMEM((4, 4, 16, 2 * q), BF),
        pltpu.VMEM((3, 4, 16, q), BF),
        pltpu.VMEM((3, 4, 16, q), BF),
        pltpu.VMEM((4, 16, q), BF),
        pltpu.VMEM((4, 16, q), BF),
        pltpu.VMEM((3, 16, q), BF),
        pltpu.VMEM((3, 16, q), BF),
        pltpu.VMEM((16, 2 * q), BF),
        pltpu.VMEM((3, 16, 2 * q), BF),
        pltpu.VMEM((2, 16, 2 * q), F32),
    ]


def local(volume, w_first, w_second, cotangent):
    w1 = jnp.swapaxes(w_first, 3, 4).reshape(27, 16, 128)
    w2 = jnp.swapaxes(w_second, 3, 4).reshape(27, 16, 256)
    cotl = jnp.transpose(cotangent, (2, 4, 1, 0, 3)).reshape(16, 16, 128)
    cotl = jnp.pad(cotl, ((0, 1), (0, 0), (0, 0)))
    vmem = pl.BlockSpec(memory_space=pltpu.VMEM)
    so, vg, g1, g2 = pl.pallas_call(
        kernel,
        out_shape=(
            jax.ShapeDtypeStruct((16, 16, 128), BF),
            jax.ShapeDtypeStruct((4, 8, 4, 64, 128), BF),
            jax.ShapeDtypeStruct((27, 16, 128), F32),
            jax.ShapeDtypeStruct((27, 16, 256), F32),
        ),
        in_specs=[pl.BlockSpec(memory_space=pl.ANY), vmem, vmem, vmem],
        out_specs=(vmem, vmem, vmem, vmem),
        scratch_shapes=[
            pltpu.VMEM((4, 9, 5, 64, 128), BF),
            pltpu.VMEM((2, 2, 4, 4, 32, 1792), BF),
            pltpu.VMEM((2, 2, 4, 16, 3584), BF),
            pltpu.VMEM((2, 4, 4, 16, 1792), BF),
            pltpu.VMEM((2, 4, 4, 16, 3584), BF),
            pltpu.VMEM((2, 16, 1792), BF),
            pltpu.VMEM((2, 16, 3584), BF),
            pltpu.VMEM((2, 4, 4, 32, 256), F32),
            pltpu.VMEM((2, 4, 4, 2, 32, 128), F32),
            pltpu.VMEM((3, 5, 4, 32, 256), BF),
            pltpu.VMEM((3, 5, 4, 32, 256), BF),
            pltpu.VMEM((3, 5, 4, 32, 256), BF),
            pltpu.VMEM((2, 4, 256, 128), BF),
            pltpu.VMEM((2, 16, 16, 128), BF),
            pltpu.VMEM((2, 3, 4, 16, 256), BF),
            pltpu.VMEM((2, 3, 4, 16, 256), BF),
            pltpu.VMEM((5, 72, 128), F32),
            pltpu.VMEM((5, 40, 256), F32),
            pltpu.VMEM((8, 64, 128), F32),
            *sums(896),
            *sums(1792),
            pltpu.VMEM((16, 16, 128), BF),
            pltpu.VMEM((16, 16, 128), BF),
            pltpu.SemaphoreType.DMA((NSEM,)),
            pltpu.SemaphoreType.DMA((NSEM,)),
            pltpu.SemaphoreType.DMA((1,)),
        ],
        compiler_params=pltpu.CompilerParams(
            collective_id=0, has_side_effects=True, vmem_limit_bytes=60 * 1024 * 1024
        ),
        cost_estimate=pl.CostEstimate(flops=6_800_000_000, bytes_accessed=6_000_000, transcendentals=0),
        name="two_layers",
    )(volume, w1, w2, cotl)
    so = jnp.transpose(so.reshape(16, 16, 2, 4, 16), (3, 2, 0, 4, 1))
    g1 = jnp.swapaxes(g1.reshape(3, 3, 3, 16, 128), 3, 4)
    g2 = jnp.swapaxes(g2.reshape(3, 3, 3, 16, 256), 3, 4)
    return so, vg, g1, g2


def solution(mesh):
    space, chan = ("y", "core"), ("z", "x")
    finer = Mesh(mesh.devices.reshape(4, 2, 4, 4), (*space, *chan))
    return jax.shard_map(
        local,
        mesh=finer,
        in_specs=(
            P(None, space, chan, None, None),
            P(None, None, None, None, chan),
            P(None, None, None, None, chan),
            P(None, space, None, None, chan),
        ),
        out_specs=(
            P(None, space, None, None, chan),
            P(None, space, chan, None, None),
            P(None, None, None, None, chan),
            P(None, None, None, None, chan),
        ),
        check_vma=False,
    )
```

time: 329 us -> 105 us (0.32); the launches traced: 323 us -> 105 us
  local copies, waits for them, and re-layouts: 126 us -> 9.42 us
  Pallas kernels: 0 us -> 94.9 us
  waiting for transfers between devices: 72.2 us -> 0 us
  starting transfers between devices: 54.4 us -> 0 us
  matrix products: 27.4 us -> 0 us
  between operations: 16.4 us -> 0.66 us
  blocking collectives: 14.7 us -> 0 us
  other arithmetic: 11.6 us -> 0 us
    pallas_call x0 -> x1, Pallas kernels: none -> 94.9 us  [local(): pl.pallas_call(kernel, out_shape=(jax.ShapeDtypeStruct((16, 16, 128), BF)...]
    scatter-add x1 -> x0, local copies, waits for them, and re-layouts: 61.1 us -> none  [local(): grad_fold = grad_fold.at[:, :, -1:].add(row_grad)]
    reduce_scatter x2 -> x0, waiting for transfers between devices: 33.8 us -> none  [scatter_axes(): array = lax.psum_scatter(array, axis, scatter_dimension=dim, tiled=True)]
    ppermute x8 -> x0, waiting for transfers between devices: 28.8 us -> none  [from_behind(): lax.ppermute(value, axis, [(source, source + steps) for source in range(f...]
    all_to_all x5 -> x0, starting transfers between devices: 28.6 us -> none  [the longest x3 15.9 us: from_everyone(): lax.all_to_all(jnp.broadcast_to(array[None], (peers, *array.shape)), axis...]
    ppermute x8 -> x0, starting transfers between devices: 25.3 us -> none  [from_behind(): lax.ppermute(value, axis, [(source, source + steps) for source in range(f...]
    conv_general_dilated x4 -> x0, matrix products: 18.5 us -> none  [the longest x2 12 us: input_grad(): lax.conv_general_dilated(grad_cells, flipped, (1, 1, 1), ((2, 2), (2, 2),...]
    all_to_all x1 -> x0, blocking collectives: 14.7 us -> none  [local(): lax.all_to_all(cotangent, CHAN, split_axis=2, concat_axis=4, tiled=True)]
  transfers between devices with their start and end apart: 16 -> 0, of which waited for: 10 -> 0; matrix products, arithmetic and copies ran while one was open for 46% -> 0% of each run, Pallas kernels for 0% -> 0%
where the time goes in v1:
time: 105 us
  Pallas kernels  94.9 us (90%)
  local copies, waits for them, and re-layouts  9.42 us (9%)
    pallas_call x1, Pallas kernels, local(): pl.pallas_call(kernel, out_shape=(jax.ShapeDtypeStruct((16, 16, 128), BF)...  94.9 us
    unnamed x7, local copies, waits for them, and re-layouts  4.71 us
    reshape x2, local copies, waits for them, and re-layouts, local(): so = jnp.transpose(so.reshape(16, 16, 2, 4, 16), (3, 2, 0, 4, 1))  2.37 us

profile of v1, /device:TPU:1, one launch (start us, length us, event | category | flops | bytes accessed | tf_op | source)
XLA Modules:
  0.0 105.0 jit_solution(6033202148927497622)
XLA Ops:
  0.6 1.4 %copy.8 = bf16[16,16,2,4,16]{4,3,2,1,0:T(4,128)(2,1)S(1)} copy(bf16[16,16,2,4,16]{1,4,0,2,3:T(8,128)(2,1)} %bitcast.14) | data formatting | bytes 131072 | tf_op jit(solution)/shard_map/transpose | solution.py:480
  2.0 0.3 reshape.28
  2.4 0.6 pad.4.cotl
  3.0 94.9 %two_layers.1 = (bf16[16,16,128]{2,1,0:T(8,128)(2,1)}, bf16[4,8,4,64,128]{4,3,2,1,0:T(8,128)(2,1)}, f32[27,16,128]{2,1,0:T(8,128)}, f32[27,16,256]{2,1,0:T(8,128)}) custom-call(bf16[4,8,4,64,128]{4,3,2,1,0:T(8,128)(2,1)} %vol.1, bf16[27,16,128]{2,1,0:T(8,128)(2,1)} %bitcast.19, bf16[27,16,256]{2,1,0:T(8,128)(2,1)} %bitcast.18, bf16[17,16,128]{2,1,0:T(8,128)(2,1)} %pad.4.cotl), custom_call_target="tpu_custom_call" | custom-call | flops 6800000000 | bytes 6000000 | tf_op jit(solution)/shard_map/two_layers/pallas_call | solution.py:483
  97.9 1.2 %reshape.29 = bf16[16,16,2,4,16]{4,3,2,1,0:T(4,128)(2,1)S(1)} reshape(bf16[16,16,128]{2,1,0:T(8,128)(2,1)} %get-tuple-element.8) | data formatting | bytes 131072 | tf_op jit(solution)/shard_map/reshape | solution.py:527
  99.1 1.2 %copy.9 = bf16[16,16,2,4,16]{1,4,0,2,3:T(8,128)(2,1)} copy(bf16[16,16,2,4,16]{4,3,2,1,0:T(4,128)(2,1)S(1)} %reshape.29) | data formatting | bytes 131072 | tf_op jit(solution)/shard_map/reshape | solution.py:527
  100.3 0.0 copy-start.1
  100.3 0.0 copy-start
  100.3 3.3 %copy.13 = bf16[4,8,4,64,128]{4,3,2,1,0:T(8,128)(2,1)} copy(bf16[4,8,4,64,128]{4,3,2,1,0:T(8,128)(2,1)} %get-tuple-element.17) | data formatting | bytes 4194304
  103.6 0.0 copy-done.1
  103.6 0.7 copy.14
  104.3 0.0 copy-done
  104.3 0.8 copy.15
Async XLA Ops:
  100.3 3.3 %copy-start.1 = (f32[27,16,128]{2,1,0:T(8,128)S(1)}, f32[27,16,128]{2,1,0:T(8,128)}, u32[]{:S(2)}) copy-start(f32[27,16,128]{2,1,0:T(8,128)} %get-tuple-element.10) | copy-start | bytes 663556
  100.3 3.9 %copy-start = (f32[27,16,256]{2,1,0:T(8,128)S(1)}, f32[27,16,256]{2,1,0:T(8,128)}, u32[]{:S(2)}) copy-start(f32[27,16,256]{2,1,0:T(8,128)} %get-tuple-element.11) | copy-start | bytes 1327108

commit v2 on v1

--- a/solution.py
+++ b/solution.py
@@ -9,7 +9,7 @@
 MESH = pl.DeviceIdType.MESH
 BF = jnp.bfloat16
 F32 = jnp.float32
-NSEM = 128
+NSEM = 160
 
 SLOT = {}
 for _g in range(9):
@@ -46,12 +46,12 @@
 
 
 def kernel(
-    vol, w1, w2, cotl, so, vg, g1, g2,
-    xv, im1, im2, wf1, wf2, w1o, w2o, pre, ab, hid, pb0, pb1, pbt, cott, cot0, cot1, fa, fb, vs,
-    g1o, g1s, g1r, c1, r1a, r1b, s1a, s1b, q1a, q1b, t1, y1, f1,
-    g2o, g2s, g2r, c2, r2a, r2b, s2a, s2b, q2a, q2b, t2, y2, f2,
-    ot, sor, ssem, rsem, lsem,
+    vol, w1, w2, cot, so, vg, g1, g2,
+    xv, im1, im2, wf1, wf2, w1o, w2o, pre, ab, hid, pb0, pb1, pbt, cotv, cotl, cott, cot0, cot1, fa, vs,
+    *rest,
 ):
+    sums1, sums2 = rest[:NSUM], rest[NSUM : 2 * NSUM]
+    ot, relay, ssem, rsem, lsem, hsend, hrecv = rest[2 * NSUM :]
     y, core = lax.axis_index("y"), lax.axis_index("core")
     z, x = lax.axis_index("z"), lax.axis_index("x")
     chan = z * 4 + x
@@ -81,21 +81,26 @@
         sent.append(copy)
         return copy
 
+    class hold:
+        def __init__(self, src, dst, dev):
+            n = count[0]
+            count[0] += 1
+            self.send, self.recv = hsend.at[n], hrecv.at[n]
+            self.copy = pltpu.make_async_remote_copy(
+                src_ref=src, dst_ref=dst, send_sem=self.send, recv_sem=self.recv,
+                device_id=dev, device_id_type=MESH,
+            )
+
+    count = [0]
+
     def arrived(copies):
         for copy in copies:
             copy.wait_recv()
 
+    cells = pltpu.make_async_copy(cot, cotv, lsem.at[1])
+    cells.start()
     local = pltpu.make_async_copy(vol, xv.at[:, 1:9, 1:5], lsem.at[0])
     local.start()
-
-    for tap in range(27):
-        h, l = slot(tap)
-        w1o[h, :, l * 128 : (l + 1) * 128] = w1[tap]
-        w2o[h, :, l * 256 : (l + 1) * 256] = w2[tap]
-    w1o[1, :, 13 * 128 :] = jnp.zeros((16, 128), BF)
-    w2o[1, :, 13 * 256 :] = jnp.zeros((16, 256), BF)
-    wf1[core, z, x] = w1o[core]
-    wf2[core, z, x] = w2o[core]
 
     barrier = pltpu.get_barrier_semaphore()
     partners = [chan_at(o) for o in range(1, 16)]
@@ -104,34 +109,54 @@
     partners += [{**space_at(1), **chan_at(1)}, {**space_at(7), **chan_at(15)}]
     for dev in partners:
         pl.semaphore_signal(barrier, inc=1, device_id=dev, device_id_type=MESH)
+
+    for tap in range(27):
+        h, l = slot(tap)
+        w1o[h, :, l * 128 : (l + 1) * 128] = w1[tap]
+        w2o[h, :, l * 256 : (l + 1) * 256] = w2[tap]
+    w1o[1, :, 13 * 128 :] = jnp.zeros((16, 128), BF)
+    w2o[1, :, 13 * 256 :] = jnp.zeros((16, 256), BF)
+    for own, full, e in ((w1o, wf1, 128), (w2o, wf2, 256)):
+        at = pl.ds(pl.multiple_of(y * 2 * e, 2 * e), 2 * e)
+        full[core, z, x, :, at] = own[core, :, at]
+        full[core, z, x, :, 8 * e :] = own[core, :, 8 * e :]
+
     pl.semaphore_wait(barrier, len(partners))
 
-    def spread_first(own, full, q):
-        a = [put(own.at[core, :, pl.ds(0, q)], full.at[core, z, x, :, pl.ds(0, q)], along("x", x, o)) for o in (1, 2, 3)]
-        b = [put(own.at[core, :, pl.ds(q, q)], full.at[core, z, x, :, pl.ds(q, q)], along("z", z, o)) for o in (1, 2, 3)]
-        return a, b
-
-    def spread_second(full, q, first):
-        arrived(first[0])
-        part = full.at[core, z, :, :, pl.ds(0, q)]
-        a = [put(part, part, along("z", z, o)) for o in (1, 2, 3)]
-        arrived(first[1])
-        part = full.at[core, :, x, :, pl.ds(q, q)]
-        b = [put(part, part, along("x", x, o)) for o in (1, 2, 3)]
-        return a, b
-
-    def spread_third(full, second):
-        arrived(second[0])
-        arrived(second[1])
-        return put(full.at[core], full.at[core], sib)
-
-    w1_first = spread_first(w1o, wf1, 896)
-    vol_halo = [
-        put(vol.at[:, :, 3], xv.at[:, 1:9, 0], chan_at(1)),
-        put(vol.at[:, 7], xv.at[:, 0, 1:5], space_at(1)),
-        put(vol.at[:, 7, 3], xv.at[:, 0, 0], {**space_at(1), **chan_at(1)}),
-    ]
-    w2_first = spread_first(w2o, wf2, 1792)
+    def cut(e):
+        q = 2 * e
+        return pl.ds(pl.multiple_of(y * q, q), q), pl.ds(8 * e, 4 * e), pl.ds(12 * e, 2 * e)
+
+    def one_row(own, full, at, name):
+        me = x if name == "x" else z
+        return [put(own.at[core, :, at], full.at[core, z, x, :, at], along(name, me, o)) for o in (1, 2, 3)]
+
+    def four_rows(full, at, name, before):
+        arrived(before)
+        part = full.at[core, z, :, :, at] if name == "z" else full.at[core, :, x, :, at]
+        return [put(part, part, along(name, x if name == "x" else z, o)) for o in (1, 2, 3)]
+
+    def all_rows(full, at, before):
+        arrived(before)
+        part = full.at[core, :, :, :, at]
+        return [put(part, part, along("y", y, o)) for o in (1, 2, 3)]
+
+    def spread_last(full, at, copies):
+        arrived(copies)
+        part = full.at[core, :, :, :, at]
+        return put(part, part, sib)
+
+    (p1, q1, r1), (p2, q2, r2) = cut(128), cut(256)
+    w1_px, w1_qx, w1_rz = one_row(w1o, wf1, p1, "x"), one_row(w1o, wf1, q1, "x"), one_row(w1o, wf1, r1, "z")
+    w2_px, w2_rz, w2_qx = one_row(w2o, wf2, p2, "x"), one_row(w2o, wf2, r2, "z"), one_row(w2o, wf2, q2, "x")
+    vol_plane = put(vol.at[:, 7], xv.at[:, 0, 1:5], space_at(1))
+
+    cells.wait()
+    unit = (lax.broadcasted_iota(jnp.int32, (16, 16), 0) == lax.broadcasted_iota(jnp.int32, (16, 16), 1)).astype(BF)
+    for b in range(16):
+        row = jnp.concatenate([cotv[v, a, b] for a in range(2) for v in range(4)], axis=0)
+        cotl[b] = dot_nt(unit, row).astype(BF)
+    cotl[16] = jnp.zeros((16, 128), BF)
     cots = []
     for o in range(1, 16):
         dev = chan_at(o)
@@ -139,8 +164,33 @@
         cots.append(put(cotl.at[pl.ds(row, 2)], cott.at[:, chan], dev))
     cott[:, chan] = cotl[pl.ds(chan, 2)]
 
+    w1_pz = four_rows(wf1, p1, "z", w1_px)
+    w2_pz = four_rows(wf2, p2, "z", w2_px)
+    w1_qz = four_rows(wf1, q1, "z", w1_qx)
+    w1_rx = four_rows(wf1, r1, "x", w1_rz)
+
+    vol_row = [
+        put(vol.at[0:2, :, 3], xv.at[0:2, 1:9, 0], chan_at(1)),
+        put(vol.at[:, 7, 3], xv.at[:, 0, 0], {**space_at(1), **chan_at(1)}),
+    ]
+    vol_step, vol_half = hold(vol.at[2:4, :, 3], relay, {"z": lax.rem(z + 1, 4)}), hold(vol.at[2:4, :, 3], xv.at[2:4, 1:9, 0], chan_at(1))
+    vol_on = pltpu.make_async_remote_copy(
+        src_ref=relay, dst_ref=xv.at[2:4, 1:9, 0], send_sem=vol_half.send, recv_sem=vol_half.recv,
+        device_id=along("x", x, 1), device_id_type=MESH,
+    )
+
+    @pl.when(x == 3)
+    def _():
+        vol_step.copy.start()
+
+    @pl.when(x != 3)
+    def _():
+        vol_half.copy.start()
+
+    w2_rx = four_rows(wf2, r2, "x", w2_rz)
+    w2_qz = four_rows(wf2, q2, "z", w2_qx)
+
     fa[:, 0:8, :] = jnp.zeros((5, 8, 128), F32)
-    fb[:, 0:8, :] = jnp.zeros((5, 8, 256), F32)
 
     def patches(blocks):
         def body(v):
@@ -164,31 +214,30 @@
     im2[1, :, :, :, 13 * 256 :] = jnp.zeros((2, 4, 16, 256), BF)
     local.wait()
     patches([(a, b) for a in range(1, 9) for b in range(1, 5)])
-
-    w1_second = spread_second(wf1, 896, w1_first)
-    w2_second = spread_second(wf2, 1792, w2_first)
+    w1_py = all_rows(wf1, p1, w1_pz)
+    w2_py = all_rows(wf2, p2, w2_pz)
+
+    @pl.when(x == 3)
+    def _():
+        vol_step.copy.wait()
+        vol_on.start()
 
     arrived(cots)
-    last = lax.broadcasted_iota(jnp.int32, (64, 256), 0) % 16 == 15
     for b in range(2):
         rows = cott[b].reshape(256, 128).astype(F32).T.astype(BF)
         cot0[b, 0:2] = rows.reshape(2, 4, 16, 256)
     cot_halo = put(cot0.at[:, 0], cot0.at[:, 2], space_at(7))
 
-    arrived(vol_halo)
-
-    @pl.when(chan == 0)
-    def _():
-        xv[:, :, 0] = jnp.zeros((4, 9, 64, 128), BF)
+    arrived([vol_plane])
 
     @pl.when(space == 0)
     def _():
-        xv[:, 0] = jnp.zeros((4, 5, 64, 128), BF)
-
-    patches([(a, 0) for a in range(9)] + [(0, b) for b in range(1, 5)])
-
-    w1_third = spread_third(wf1, w1_second)
-    arrived([w1_third])
+        xv[:, 0, 1:5] = jnp.zeros((4, 4, 64, 128), BF)
+
+    patches([(0, b) for b in range(1, 5)])
+
+    w1_last = [spread_last(wf1, pl.ds(1024, 768), w1_qz + w1_rx), spread_last(wf1, pl.ds(0, 1024), w1_py)]
+    arrived(w1_last)
 
     def conv_first(q):
         def body(n):
@@ -206,9 +255,6 @@
         put(hid.at[2, 1:5], hid.at[0, 1:5], chan_at(1)),
         put(hid.at[2, 4], hid.at[0, 0], {**space_at(1), **chan_at(1)}),
     ]
-    w2_third = spread_third(wf2, w2_second)
-    conv_first(0)
-    hid_halo.append(put(hid.at[1:3, 4], hid.at[1:3, 0], space_at(1)))
 
     arrived([cot_halo])
 
@@ -216,13 +262,29 @@
     def _():
         cot0[:, 2] = jnp.zeros((2, 4, 16, 256), BF)
 
+    last = lax.broadcasted_iota(jnp.int32, (64, 256), 0) % 16 == 15
     for b in range(2):
         for a in range(3):
             rows = cot0[b, a].reshape(64, 256).astype(F32)
             rows = jnp.where(last, 0.0, pltpu.roll(rows, 63, 0))
             cot1[b, a] = rows.astype(BF).reshape(4, 16, 256)
 
-    arrived([w2_third])
+    arrived(vol_row)
+    vol_half.copy.wait_recv()
+
+    @pl.when(chan == 0)
+    def _():
+        xv[:, :, 0] = jnp.zeros((4, 9, 64, 128), BF)
+
+    @pl.when(space == 0)
+    def _():
+        xv[:, 0, 0] = jnp.zeros((4, 64, 128), BF)
+
+    patches([(a, 0) for a in range(9)])
+    conv_first(0)
+    hid_halo.append(put(hid.at[1:3, 4], hid.at[1:3, 0], space_at(1)))
+    w2_last = [spread_last(wf2, pl.ds(2048, 1536), w2_qz + w2_rx), spread_last(wf2, pl.ds(0, 2048), w2_py)]
+    arrived(w2_last)
 
     cot_at = (cot0, cot1)
     for s1 in range(2):
@@ -258,19 +320,6 @@
         put(pb0.at[0, 0], pb0.at[2, 4], {**space_at(7), **chan_at(15)}),
     ]
 
-    def first_filters(half, dst, kind):
-        lhs = jnp.concatenate([pbt[q, p] for q in range(2) for p in range(4)], axis=1)
-
-        def body(n):
-            at = pl.ds(pl.multiple_of(n * 256, 256), 256)
-            dst[:, at] = dot(lhs, im1[half, :, :, :, :, at].reshape(1024, 256)).astype(kind)
-
-        loop(7, body)
-
-    first_filters(1 - core, g1s, BF)
-    g1_pair = put(g1s, g1r, sib)
-    first_filters(core, g1o, F32)
-
     arrived(hid_halo)
 
     @pl.when(chan == 0)
@@ -306,72 +355,127 @@
 
         loop(7, body)
 
-    second_filters(1 - core, g2s, BF)
-    g2_pair = put(g2s, g2r, sib)
-    second_filters(core, g2o, F32)
-
-    def sum_pair(pair, own, other, chip, q):
-        arrived([pair])
+    def first_filters(half, dst, kind):
+        lhs = jnp.concatenate([pbt[q, p] for q in range(2) for p in range(4)], axis=1)
 
         def body(n):
-            at = pl.ds(pl.multiple_of(n * 16, 16), 16)
-            total = own[at] + other[at].astype(F32)
-            chip[lax.div(n, 4), lax.rem(n, 4)] = total.astype(BF)
-
-        loop(16, body)
-
-    def sum_first(chip, ra, rb, q):
-        a, b = [], []
-        for o in (1, 2, 3):
-            to = lax.rem(z + o, 4)
-            a.append(put(chip.at[to, :, :, pl.ds(0, q)], ra.at[o - 1], {"z": to}))
-            to = lax.rem(x + o, 4)
-            b.append(put(chip.at[:, to, :, pl.ds(q, q)], rb.at[o - 1], {"x": to}))
-        return a, b
-
-    def sum_second(chip, ra, rb, sa, sb, qa, qb, q, first):
-        arrived(first[0])
-        total = chip[z, :, :, 0:q].astype(F32)
-        for o in range(3):
-            total += ra[o].astype(F32)
-        sa[...] = total.astype(BF)
-        a, b = [], []
-        for o in (1, 2, 3):
-            to = lax.rem(x + o, 4)
-            a.append(put(sa.at[to], qa.at[o - 1], {"x": to}))
-        arrived(first[1])
-        total = chip[:, x, :, q : 2 * q].astype(F32)
-        for o in range(3):
-            total += rb[o].astype(F32)
-        sb[...] = total.astype(BF)
-        for o in (1, 2, 3):
-            to = lax.rem(z + o, 4)
-            b.append(put(sb.at[to], qb.at[o - 1], {"z": to}))
-        return a, b
-
-    def sum_third(sa, sb, qa, qb, t, yr, q, second):
-        arrived(second[0])
-        total = sa[x].astype(F32)
-        for o in range(3):
-            total += qa[o].astype(F32)
-        t[:, 0:q] = total.astype(BF)
-        arrived(second[1])
-        total = sb[z].astype(F32)
-        for o in range(3):
-            total += qb[o].astype(F32)
-        t[:, q : 2 * q] = total.astype(BF)
-        return [put(t, yr.at[o - 1], along("y", y, o)) for o in (1, 2, 3)]
-
-    def sum_last(t, yr, f, third):
-        arrived(third)
-        total = t[...].astype(F32)
-        for o in range(3):
-            total += yr[o].astype(F32)
-        f[core] = total
-        return put(f.at[core], f.at[core], sib)
-
-    sum_pair(g1_pair, g1o, g1r, c1, 896)
-    g1_first = sum_first(c1, r1a, r1b, 896)
+            at = pl.ds(pl.multiple_of(n * 256, 256), 256)
+            dst[:, at] = dot(lhs, im1[half, :, :, :, :, at].reshape(1024, 256)).astype(kind)
+
+        loop(7, body)
+
+    class Sum:
+        def __init__(self, refs, e):
+            self.e = e
+            (self.own, self.out, self.other, self.chip, self.yr, self.ys, self.fin) = refs[:7]
+            self.recv = refs[7:10], refs[10:13], refs[13:16]
+            self.yq, self.yp, self.full = refs[16:19]
+            w = [e, 5 * e, 5 * e]
+            self.width = w
+            self.begin = [0, 4 * e, 9 * e]
+            self.order = "zx", "zx", "xz"
+
+        def pair(self, filters):
+            filters(1 - core, self.out, BF)
+            self.link = put(self.out, self.other, sib)
+
+        def start(self):
+            arrived([self.link])
+
+            def body(n):
+                at = pl.ds(pl.multiple_of(n * 16, 16), 16)
+                total = self.own[at] + self.other[at].astype(F32)
+                self.chip[lax.div(n, 4), lax.rem(n, 4)] = total.astype(BF)
+
+            loop(16, body)
+            e = self.e
+            self.copies = []
+            for o in (1, 2, 3):
+                to = lax.rem(y + o, 4)
+                at = pl.ds(pl.multiple_of(to * e, e), e)
+                self.copies.append(put(self.chip.at[:, :, :, at], self.yr.at[o - 1], {"y": to}))
+            self.first = [None, self.send_first(1), self.send_first(2)]
+
+        def source(self, part):
+            if part == 0:
+                return self.ys, pl.ds(0, self.e)
+            return self.chip, pl.ds(self.begin[part], self.width[part])
+
+        def send_first(self, part):
+            src, at = self.source(part)
+            name, me = ("z", z) if self.order[part][0] == "z" else ("x", x)
+            out = []
+            for o in (1, 2, 3):
+                to = lax.rem(me + o, 4)
+                view = src.at[to, :, :, at] if name == "z" else src.at[:, to, :, at]
+                out.append(put(view, self.recv[part][0].at[o - 1], {name: to}))
+            return out
+
+        def shared(self):
+            arrived(self.copies)
+            e = self.e
+            at = pl.ds(pl.multiple_of(y * e, e), e)
+
+            def body(n):
+                total = self.chip[n, :, :, at].astype(F32)
+                for o in range(3):
+                    total += self.yr[o, n].astype(F32)
+                self.ys[n] = total.astype(BF)
+
+            loop(4, body)
+            self.first[0] = self.send_first(0)
+
+        def second(self, part):
+            arrived(self.first[part])
+            src, at = self.source(part)
+            got, mid, _ = self.recv[part]
+            total = (src[z, :, :, at] if self.order[part][0] == "z" else src[:, x, :, at]).astype(F32)
+            for o in range(3):
+                total += got[o].astype(F32)
+            mid[...] = total.astype(BF)
+            name, me = ("x", x) if self.order[part][0] == "z" else ("z", z)
+            out = []
+            for o in (1, 2, 3):
+                to = lax.rem(me + o, 4)
+                out.append(put(mid.at[to], self.recv[part][2].at[o - 1], {name: to}))
+            self.first[part] = out
+
+        def third(self, part):
+            arrived(self.first[part])
+            _, mid, got = self.recv[part]
+            total = (mid[x] if self.order[part][0] == "z" else mid[z]).astype(F32)
+            for o in range(3):
+                total += got[o].astype(F32)
+            e = self.e
+            if part == 0:
+                self.fin[y] = total.astype(BF)
+                self.last0 = [put(self.fin.at[y], self.fin.at[y], along("y", y, o)) for o in (1, 2, 3)]
+            else:
+                at = slice((part - 1) * 5 * e, part * 5 * e)
+                self.yq[:, at] = total.astype(BF)
+
+        def fourth(self):
+            self.last1 = [put(self.yq, self.yp.at[o - 1], along("y", y, o)) for o in (1, 2, 3)]
+
+        def final(self):
+            e = self.e
+            arrived(self.last0)
+            for n in range(4):
+                self.full[core, :, n * e : (n + 1) * e] = self.fin[n].astype(F32)
+            arrived(self.last1)
+            total = self.yq[...].astype(F32)
+            for o in range(3):
+                total += self.yp[o].astype(F32)
+            self.full[core, :, 4 * e : 14 * e] = total
+            self.done = put(self.full.at[core], self.full.at[core], sib)
+
+    sum1, sum2 = Sum(sums1, 128), Sum(sums2, 256)
+    sum2.pair(second_filters)
+    second_filters(core, sum2.own, F32)
+    sum1.pair(first_filters)
+    sum2.start()
+    first_filters(core, sum1.own, F32)
+    sum1.start()
 
     total = jnp.zeros((256, 128), F32)
     for h in range(2):
@@ -380,11 +484,9 @@
     outs = []
     for o in range(1, 16):
         dev = chan_at(o)
-        outs.append(put(ot.at[dev["z"] * 4 + dev["x"]], sor.at[chan], dev))
-    sor[chan] = ot[chan]
-
-    sum_pair(g2_pair, g2o, g2r, c2, 1792)
-    g2_first = sum_first(c2, r2a, r2b, 1792)
+        outs.append(put(ot.at[dev["z"] * 4 + dev["x"]], so.at[chan], dev))
+    so[chan] = ot[chan]
+    sum2.shared()
 
     arrived(pb_halo)
 
@@ -405,7 +507,6 @@
             pb1[q, p] = rows.astype(BF).reshape(4, 32, 256)
 
     loop(3, shifted)
-    g1_second = sum_second(c1, r1a, r1b, s1a, s1b, q1a, q1b, 896, g1_first)
 
     def volume_grad(q):
         def body(n):
@@ -436,59 +537,97 @@
         loop(2, body)
 
     volume_grad(0)
-    g1_third = sum_third(s1a, s1b, q1a, q1b, t1, y1, 896, g1_second)
-    g2_second = sum_second(c2, r2a, r2b, s2a, s2b, q2a, q2b, 1792, g2_first)
+    sum1.shared()
+    sum2.second(1)
+    sum2.second(2)
+    sum2.second(0)
     volume_grad(1)
-    g1_last = sum_last(t1, y1, f1, g1_third)
-    g2_third = sum_third(s2a, s2b, q2a, q2b, t2, y2, 1792, g2_second)
+    sum1.second(1)
+    sum1.second(2)
+    sum1.second(0)
+    for part in (1, 2):
+        sum2.third(part)
+    sum2.fourth()
+    sum2.third(0)
+    for part in (1, 2):
+        sum1.third(part)
+    sum1.fourth()
+    sum1.third(0)
     arrived(outs)
-    so[...] = sor[...]
-    arrived([g1_last])
+    sum2.final()
+    sum1.final()
+    arrived([sum2.done])
+    for h in range(2):
+        g2[h] = sum2.full[h]
+    arrived([sum1.done])
+    for h in range(2):
+        g1[h] = sum1.full[h]
+    for copy in sent:
+        copy.wait_send()
+    vol_half.copy.wait_send()
+
+
+def finish(so, vg, g1, g2, so_out, vg_out, g1_out, g2_out, held, sem):
+    loads = [pltpu.make_async_copy(vg.at[v], held.at[v], sem.at[0, v]) for v in range(4)]
+    stores = [pltpu.make_async_copy(held.at[v], vg_out.at[v], sem.at[1, v]) for v in range(4)]
+    for copy in loads:
+        copy.start()
+    for v in range(4):
+        loads[v].wait()
+        stores[v].start()
+    rows = so[...].reshape(256, 128).astype(F32).T.astype(BF)
+    for b in range(16):
+        for a in range(2):
+            for v in range(4):
+                n = (a * 4 + v) * 16
+                so_out[v, a, b] = rows[n : n + 16, 16 * b : 16 * b + 16]
     for tap in range(27):
         h, l = slot(tap)
-        g1[tap] = f1[h, :, l * 128 : (l + 1) * 128]
-    g2_last = sum_last(t2, y2, f2, g2_third)
-    arrived([g2_last])
-    for tap in range(27):
-        h, l = slot(tap)
-        g2[tap] = f2[h, :, l * 256 : (l + 1) * 256]
-    for copy in sent:
-        copy.wait_send()
-
-
-def sums(q):
+        g1_out[tap] = g1[h, :, l * 128 : (l + 1) * 128]
+        g2_out[tap] = g2[h, :, l * 256 : (l + 1) * 256]
+    for copy in stores:
+        copy.wait()
+
+
+NSUM = 19
+
+
+def sums(e):
+    per_part = []
+    for width, part in ((e, 0), (5 * e, 1), (5 * e, 2)):
+        per_part += [
+            pltpu.VMEM((3, 4, 16, width), BF),
+            pltpu.VMEM((4, 16, width), BF),
+            pltpu.VMEM((3, 16, width), BF),
+        ]
     return [
-        pltpu.VMEM((256, 2 * q), F32),
-        pltpu.VMEM((256, 2 * q), BF),
-        pltpu.VMEM((256, 2 * q), BF),
-        pltpu.VMEM((4, 4, 16, 2 * q), BF),
-        pltpu.VMEM((3, 4, 16, q), BF),
-        pltpu.VMEM((3, 4, 16, q), BF),
-        pltpu.VMEM((4, 16, q), BF),
-        pltpu.VMEM((4, 16, q), BF),
-        pltpu.VMEM((3, 16, q), BF),
-        pltpu.VMEM((3, 16, q), BF),
-        pltpu.VMEM((16, 2 * q), BF),
-        pltpu.VMEM((3, 16, 2 * q), BF),
-        pltpu.VMEM((2, 16, 2 * q), F32),
+        pltpu.VMEM((256, 14 * e), F32),
+        pltpu.VMEM((256, 14 * e), BF),
+        pltpu.VMEM((256, 14 * e), BF),
+        pltpu.VMEM((4, 4, 16, 14 * e), BF),
+        pltpu.VMEM((3, 4, 4, 16, e), BF),
+        pltpu.VMEM((4, 4, 16, e), BF),
+        pltpu.VMEM((4, 16, e), BF),
+        *per_part,
+        pltpu.VMEM((16, 10 * e), BF),
+        pltpu.VMEM((3, 16, 10 * e), BF),
+        pltpu.VMEM((2, 16, 14 * e), F32),
     ]
 
 
 def local(volume, w_first, w_second, cotangent):
     w1 = jnp.swapaxes(w_first, 3, 4).reshape(27, 16, 128)
     w2 = jnp.swapaxes(w_second, 3, 4).reshape(27, 16, 256)
-    cotl = jnp.transpose(cotangent, (2, 4, 1, 0, 3)).reshape(16, 16, 128)
-    cotl = jnp.pad(cotl, ((0, 1), (0, 0), (0, 0)))
-    vmem = pl.BlockSpec(memory_space=pltpu.VMEM)
+    vmem, anywhere = pl.BlockSpec(memory_space=pltpu.VMEM), pl.BlockSpec(memory_space=pl.ANY)
     so, vg, g1, g2 = pl.pallas_call(
         kernel,
         out_shape=(
             jax.ShapeDtypeStruct((16, 16, 128), BF),
             jax.ShapeDtypeStruct((4, 8, 4, 64, 128), BF),
-            jax.ShapeDtypeStruct((27, 16, 128), F32),
-            jax.ShapeDtypeStruct((27, 16, 256), F32),
+            jax.ShapeDtypeStruct((2, 16, 1792), F32),
+            jax.ShapeDtypeStruct((2, 16, 3584), F32),
         ),
-        in_specs=[pl.BlockSpec(memory_space=pl.ANY), vmem, vmem, vmem],
+        in_specs=[anywhere, vmem, vmem, anywhere],
         out_specs=(vmem, vmem, vmem, vmem),
         scratch_shapes=[
             pltpu.VMEM((4, 9, 5, 64, 128), BF),
@@ -504,27 +643,42 @@
             pltpu.VMEM((3, 5, 4, 32, 256), BF),
             pltpu.VMEM((3, 5, 4, 32, 256), BF),
             pltpu.VMEM((2, 4, 256, 128), BF),
+            pltpu.VMEM((4, 2, 16, 16, 16), BF),
+            pltpu.VMEM((17, 16, 128), BF),
             pltpu.VMEM((2, 16, 16, 128), BF),
             pltpu.VMEM((2, 3, 4, 16, 256), BF),
             pltpu.VMEM((2, 3, 4, 16, 256), BF),
             pltpu.VMEM((5, 72, 128), F32),
-            pltpu.VMEM((5, 40, 256), F32),
             pltpu.VMEM((8, 64, 128), F32),
-            *sums(896),
-            *sums(1792),
+            *sums(128),
+            *sums(256),
             pltpu.VMEM((16, 16, 128), BF),
-            pltpu.VMEM((16, 16, 128), BF),
+            pltpu.VMEM((2, 8, 64, 128), BF),
             pltpu.SemaphoreType.DMA((NSEM,)),
             pltpu.SemaphoreType.DMA((NSEM,)),
-            pltpu.SemaphoreType.DMA((1,)),
+            pltpu.SemaphoreType.DMA((2,)),
+            pltpu.SemaphoreType.DMA((2,)),
+            pltpu.SemaphoreType.DMA((2,)),
         ],
         compiler_params=pltpu.CompilerParams(
-            collective_id=0, has_side_effects=True, vmem_limit_bytes=60 * 1024 * 1024
+            collective_id=0, has_side_effects=True, vmem_limit_bytes=56 * 1024 * 1024
         ),
         cost_estimate=pl.CostEstimate(flops=6_800_000_000, bytes_accessed=6_000_000, transcendentals=0),
         name="two_layers",
-    )(volume, w1, w2, cotl)
-    so = jnp.transpose(so.reshape(16, 16, 2, 4, 16), (3, 2, 0, 4, 1))
+    )(volume, w1, w2, cotangent)
+    so, vg, g1, g2 = pl.pallas_call(
+        finish,
+        out_shape=(
+            jax.ShapeDtypeStruct((4, 2, 16, 16, 16), BF),
+            jax.ShapeDtypeStruct((4, 8, 4, 64, 128), BF),
+            jax.ShapeDtypeStruct((27, 16, 128), F32),
+            jax.ShapeDtypeStruct((27, 16, 256), F32),
+        ),
+        in_specs=[vmem, anywhere, vmem, vmem],
+        out_specs=(vmem, anywhere, vmem, vmem),
+        scratch_shapes=[pltpu.VMEM((4, 8, 4, 64, 128), BF), pltpu.SemaphoreType.DMA((2, 4))],
+        name="finish",
+    )(so, vg, g1, g2)
     g1 = jnp.swapaxes(g1.reshape(3, 3, 3, 16, 128), 3, 4)
     g2 = jnp.swapaxes(g2.reshape(3, 3, 3, 16, 256), 3, 4)
     return so, vg, g1, g2

time: 105 us -> 87.8 us (0.84)
  local copies, waits for them, and re-layouts: 9.42 us -> 0 us
  Pallas kernels: 94.9 us -> 87 us
    pallas_call x1, Pallas kernels: 94.9 us -> 82.4 us  [local(): pl.pallas_call(kernel, out_shape=(jax.ShapeDtypeStruct((16, 16, 128), BF)...]
    unnamed x7 -> x0, local copies, waits for them, and re-layouts: 4.71 us -> none
    pallas_call x0 -> x1, Pallas kernels: none -> 4.6 us  [local(): pl.pallas_call(finish, out_shape=(jax.ShapeDtypeStruct((4, 2, 16, 16, 16)...]
    reshape x3 -> x0, local copies, waits for them, and re-layouts: 2.71 us -> none  [the longest x2 2.37 us: local(): so = jnp.transpose(so.reshape(16, 16, 2, 4, 16), (3, 2, 0, 4, 1))]
    transpose x1 -> x0, local copies, waits for them, and re-layouts: 1.37 us -> none  [local(): cotl = jnp.transpose(cotangent, (2, 4, 1, 0, 3)).reshape(16, 16, 128)]
where the time goes in v2:
time: 87.8 us; the launch traced here: 87.6 us
  Pallas kernels  87 us (99%)
    pallas_call x1, Pallas kernels, local(): pl.pallas_call(kernel, out_shape=(jax.ShapeDtypeStruct((16, 16, 128), BF)...  82.4 us
    pallas_call x1, Pallas kernels, local(): pl.pallas_call(finish, out_shape=(jax.ShapeDtypeStruct((4, 2, 16, 16, 16)...  4.6 us

profile of v2, /device:TPU:1, one launch (start us, length us, event | category | flops | bytes accessed | tf_op | source)
XLA Modules:
  0.0 87.6 jit_solution(5517466765414241383)
XLA Ops:
  0.6 82.4 %two_layers.1 = (bf16[16,16,128]{2,1,0:T(8,128)(2,1)}, bf16[4,8,4,64,128]{4,3,2,1,0:T(8,128)(2,1)}, f32[2,16,1792]{2,1,0:T(8,128)}, f32[2,16,3584]{2,1,0:T(8,128)}) custom-call(bf16[4,8,4,64,128]{4,3,2,1,0:T(8,128)(2,1)} %vol.1, bf16[27,16,128]{2,1,0:T(8,128)(2,1)} %bitcast.15, bf16[27,16,256]{2,1,0:T(8,128)(2,1)} %bitcast.13, bf16[4,2,16,16,16]{4,3,2,1,0:T(8,128)(2,1)} %cot.1), custom_call_target="tpu_custom_call" | custom-call | flops 6800000000 | bytes 6000000 | tf_op jit(solution)/shard_map/two_layers/pallas_call | solution.py:622
  83.0 4.6 %finish.1 = (bf16[4,2,16,16,16]{4,3,2,1,0:T(8,128)(2,1)}, bf16[4,8,4,64,128]{4,3,2,1,0:T(8,128)(2,1)}, f32[27,16,128]{2,1,0:T(8,128)}, f32[27,16,256]{2,1,0:T(8,128)}) custom-call(bf16[16,16,128]{2,1,0:T(8,128)(2,1)} %get-tuple-element.12.so, bf16[4,8,4,64,128]{4,3,2,1,0:T(8,128)(2,1)} %get-tuple-element.13.vg, f32[2,16,1792]{2,1,0:T(8,128)} %get-tuple-element.14.g1, ...), custom_call_target="tpu_custom_call" | custom-call | tf_op jit(solution)/shard_map/finish/pallas_call | solution.py:669

commit v3 on v2

--- a/solution.py
+++ b/solution.py
@@ -51,7 +51,7 @@
     *rest,
 ):
     sums1, sums2 = rest[:NSUM], rest[NSUM : 2 * NSUM]
-    ot, relay, ssem, rsem, lsem, hsend, hrecv = rest[2 * NSUM :]
+    ot, sor, relay, ssem, rsem, lsem, hsend, hrecv = rest[2 * NSUM :]
     y, core = lax.axis_index("y"), lax.axis_index("core")
     z, x = lax.axis_index("z"), lax.axis_index("x")
     chan = z * 4 + x
@@ -116,16 +116,20 @@
         w2o[h, :, l * 256 : (l + 1) * 256] = w2[tap]
     w1o[1, :, 13 * 128 :] = jnp.zeros((16, 128), BF)
     w2o[1, :, 13 * 256 :] = jnp.zeros((16, 256), BF)
-    for own, full, e in ((w1o, wf1, 128), (w2o, wf2, 256)):
-        at = pl.ds(pl.multiple_of(y * 2 * e, 2 * e), 2 * e)
+    for own, full, q, rest_at in ((w1o, wf1, 128, 512), (w2o, wf2, 256, 1024)):
+        at = pl.ds(pl.multiple_of(y * q, q), q)
         full[core, z, x, :, at] = own[core, :, at]
-        full[core, z, x, :, 8 * e :] = own[core, :, 8 * e :]
+        full[core, z, x, :, rest_at:] = own[core, :, rest_at:]
 
     pl.semaphore_wait(barrier, len(partners))
 
-    def cut(e):
-        q = 2 * e
-        return pl.ds(pl.multiple_of(y * q, q), q), pl.ds(8 * e, 4 * e), pl.ds(12 * e, 2 * e)
+    def cut(e, shared, direct):
+        q = shared // 4 * e
+        return (
+            pl.ds(pl.multiple_of(y * q, q), q),
+            pl.ds(shared * e, direct * e),
+            pl.ds((shared + direct) * e, (14 - shared - direct) * e),
+        )
 
     def one_row(own, full, at, name):
         me = x if name == "x" else z
@@ -146,7 +150,7 @@
         part = full.at[core, :, :, :, at]
         return put(part, part, sib)
 
-    (p1, q1, r1), (p2, q2, r2) = cut(128), cut(256)
+    (p1, q1, r1), (p2, q2, r2) = cut(128, 4, 6), cut(256, 4, 6)
     w1_px, w1_qx, w1_rz = one_row(w1o, wf1, p1, "x"), one_row(w1o, wf1, q1, "x"), one_row(w1o, wf1, r1, "z")
     w2_px, w2_rz, w2_qx = one_row(w2o, wf2, p2, "x"), one_row(w2o, wf2, r2, "z"), one_row(w2o, wf2, q2, "x")
     vol_plane = put(vol.at[:, 7], xv.at[:, 0, 1:5], space_at(1))
@@ -166,8 +170,8 @@
 
     w1_pz = four_rows(wf1, p1, "z", w1_px)
     w2_pz = four_rows(wf2, p2, "z", w2_px)
+    w1_rx = four_rows(wf1, r1, "x", w1_rz)
     w1_qz = four_rows(wf1, q1, "z", w1_qx)
-    w1_rx = four_rows(wf1, r1, "x", w1_rz)
 
     vol_row = [
         put(vol.at[0:2, :, 3], xv.at[0:2, 1:9, 0], chan_at(1)),
@@ -216,7 +220,6 @@
     patches([(a, b) for a in range(1, 9) for b in range(1, 5)])
     w1_py = all_rows(wf1, p1, w1_pz)
     w2_py = all_rows(wf2, p2, w2_pz)
-
     @pl.when(x == 3)
     def _():
         vol_step.copy.wait()
@@ -236,7 +239,10 @@
 
     patches([(0, b) for b in range(1, 5)])
 
-    w1_last = [spread_last(wf1, pl.ds(1024, 768), w1_qz + w1_rx), spread_last(wf1, pl.ds(0, 1024), w1_py)]
+    w1_last = [
+        spread_last(wf1, pl.ds(0, 512), w1_py),
+        spread_last(wf1, pl.ds(512, 1280), w1_qz + w1_rx),
+    ]
     arrived(w1_last)
 
     def conv_first(q):
@@ -246,15 +252,11 @@
                 total += dot_nt(im1[h, q, pl.ds(2 * n, 2)].reshape(256, 1792), wf1[h].reshape(256, 1792))
             pre[q, pl.ds(2 * n, 2)] = total.reshape(2, 4, 32, 256)
             act = jnp.where(total > 0, total, 0.3 * total).astype(BF)
-            hid[q + 1, pl.ds(2 * n + 1, 2)] = act.reshape(2, 4, 32, 256)
+            hid[q, pl.ds(2 * n + 1, 2)] = act.reshape(2, 4, 32, 256)
 
         loop(2, body)
 
     conv_first(1)
-    hid_halo = [
-        put(hid.at[2, 1:5], hid.at[0, 1:5], chan_at(1)),
-        put(hid.at[2, 4], hid.at[0, 0], {**space_at(1), **chan_at(1)}),
-    ]
 
     arrived([cot_halo])
 
@@ -282,8 +284,163 @@
 
     patches([(a, 0) for a in range(9)])
     conv_first(0)
-    hid_halo.append(put(hid.at[1:3, 4], hid.at[1:3, 0], space_at(1)))
-    w2_last = [spread_last(wf2, pl.ds(2048, 1536), w2_qz + w2_rx), spread_last(wf2, pl.ds(0, 2048), w2_py)]
+    hid_halo = [put(hid.at[0:2, 4], hid.at[0:2, 0], space_at(1))]
+    w2_last = [spread_last(wf2, pl.ds(0, 1024), w2_py), spread_last(wf2, pl.ds(1024, 2560), w2_qz + w2_rx)]
+
+    def second_filters(half, dst, kind):
+        def body(n):
+            at = pl.ds(pl.multiple_of(n * 256, 256), 256)
+            place = half * 14 + n
+            following = jnp.int32(0)
+            for tap in range(27):
+                if tap // 3 % 3 == 0:
+                    following += jnp.where(place == SLOT[tap], 1, 0)
+            lhs = cott[following].reshape(256, 128)
+            dst[:, at] = dot(lhs, im2[half, :, :, :, at].reshape(128, 256)).astype(kind)
+
+        loop(14, body)
+
+    def first_filters(half, dst, kind):
+        lhs = jnp.concatenate([pbt[q, p] for q in range(2) for p in range(4)], axis=1)
+
+        def body(n):
+            at = pl.ds(pl.multiple_of(n * 256, 256), 256)
+            dst[:, at] = dot(lhs, im1[half, :, :, :, :, at].reshape(1024, 256)).astype(kind)
+
+        loop(7, body)
+
+    class Sum:
+        def __init__(self, refs, e):
+            self.e = e
+            (self.own, self.out, self.other, self.chip, self.yr, self.ys, self.fin) = refs[:7]
+            self.recv = refs[7:10], refs[10:13], refs[13:16]
+            self.yq, self.yp, self.full = refs[16:19]
+            w = [e, 5 * e, 5 * e]
+            self.width = w
+            self.begin = [0, 4 * e, 9 * e]
+            self.order = "zx", "zx", "xz"
+
+        def pair(self, filters):
+            filters(1 - core, self.out, BF)
+            self.link = put(self.out, self.other, sib)
+
+        def start(self):
+            arrived([self.link])
+
+            def body(n):
+                at = pl.ds(pl.multiple_of(n * 16, 16), 16)
+                total = self.own[at] + self.other[at].astype(F32)
+                self.chip[lax.div(n, 4), lax.rem(n, 4)] = total.astype(BF)
+
+            loop(16, body)
+            e = self.e
+            self.copies = []
+            for o in (1, 2, 3):
+                to = lax.rem(y + o, 4)
+                at = pl.ds(pl.multiple_of(to * e, e), e)
+                self.copies.append(put(self.chip.at[:, :, :, at], self.yr.at[o - 1], {"y": to}))
+            self.first = [None, self.send_first(1), self.send_first(2)]
+
+        def source(self, part):
+            if part == 0:
+                return self.ys, pl.ds(0, self.e)
+            return self.chip, pl.ds(self.begin[part], self.width[part])
+
+        def send_first(self, part):
+            src, at = self.source(part)
+            name, me = ("z", z) if self.order[part][0] == "z" else ("x", x)
+            out = []
+            for o in (1, 2, 3):
+                to = lax.rem(me + o, 4)
+                view = src.at[to, :, :, at] if name == "z" else src.at[:, to, :, at]
+                out.append(put(view, self.recv[part][0].at[o - 1], {name: to}))
+            return out
+
+        def shared(self):
+            arrived(self.copies)
+            e = self.e
+            at = pl.ds(pl.multiple_of(y * e, e), e)
+
+            def body(n):
+                total = self.chip[n, :, :, at].astype(F32)
+                for o in range(3):
+                    total += self.yr[o, n].astype(F32)
+                self.ys[n] = total.astype(BF)
+
+            loop(4, body)
+            self.first[0] = self.send_first(0)
+
+        def second(self, part):
+            arrived(self.first[part])
+            src, at = self.source(part)
+            got, mid, _ = self.recv[part]
+            total = (src[z, :, :, at] if self.order[part][0] == "z" else src[:, x, :, at]).astype(F32)
+            for o in range(3):
+                total += got[o].astype(F32)
+            mid[...] = total.astype(BF)
+            name, me = ("x", x) if self.order[part][0] == "z" else ("z", z)
+            out = []
+            for o in (1, 2, 3):
+                to = lax.rem(me + o, 4)
+                out.append(put(mid.at[to], self.recv[part][2].at[o - 1], {name: to}))
+            self.first[part] = out
+
+        def third(self, part):
+            arrived(self.first[part])
+            _, mid, got = self.recv[part]
+            total = (mid[x] if self.order[part][0] == "z" else mid[z]).astype(F32)
+            for o in range(3):
+                total += got[o].astype(F32)
+            e = self.e
+            if part == 0:
+                self.fin[y] = total.astype(BF)
+                self.last0 = [put(self.fin.at[y], self.fin.at[y], along("y", y, o)) for o in (1, 2, 3)]
+            else:
+                at = slice((part - 1) * 5 * e, part * 5 * e)
+                self.yq[:, at] = total.astype(BF)
+
+        def fourth(self):
+            self.last1 = [put(self.yq, self.yp.at[o - 1], along("y", y, o)) for o in (1, 2, 3)]
+
+        def final(self):
+            e = self.e
+            arrived(self.last0)
+            for n in range(4):
+                self.full[core, :, n * e : (n + 1) * e] = self.fin[n].astype(F32)
+            arrived(self.last1)
+            total = self.yq[...].astype(F32)
+            for o in range(3):
+                total += self.yp[o].astype(F32)
+            self.full[core, :, 4 * e : 14 * e] = total
+            self.done = put(self.full.at[core], self.full.at[core], sib)
+
+    sum1, sum2 = Sum(sums1, 128), Sum(sums2, 256)
+    arrived(hid_halo)
+
+    @pl.when(space == 0)
+    def _():
+        hid[:, 0] = jnp.zeros((2, 4, 32, 256), BF)
+
+    def hidden_patches(v):
+        for p in range(5):
+            for q in range(2):
+                fill = hid[q, p, v].astype(F32)
+                parts = []
+                for t in range(2):
+                    fa[p, 8:40, :] = fill[:, t * 128 : (t + 1) * 128]
+                    parts.append([fa[p, pl.ds(7 + k, 16, 2), :].astype(BF) for k in range(3)])
+                for a, i in uses(p, 2):
+                    for j in (1,) if q == 0 else (0, 2):
+                        for k in range(3):
+                            h, l = slot(9 * i + 3 * j + k)
+                            for t in range(2):
+                                im2[h, a, v, :, l * 256 + t * 128 : l * 256 + (t + 1) * 128] = parts[t][k]
+
+    loop(4, hidden_patches)
+
+    sum2.pair(second_filters)
+    second_filters(core, sum2.own, F32)
+    sum2.start()
     arrived(w2_last)
 
     cot_at = (cot0, cot1)
@@ -320,183 +477,28 @@
         put(pb0.at[0, 0], pb0.at[2, 4], {**space_at(7), **chan_at(15)}),
     ]
 
-    arrived(hid_halo)
-
-    @pl.when(chan == 0)
-    def _():
-        hid[0] = jnp.zeros((5, 4, 32, 256), BF)
-
-    @pl.when(space == 0)
-    def _():
-        hid[:, 0] = jnp.zeros((3, 4, 32, 256), BF)
-
-    def hidden_patches(v):
-        for p in range(5):
-            for j in range(3):
-                fill = hid[j, p, v].astype(F32)
-                parts = []
-                for t in range(2):
-                    fa[p, 8:40, :] = fill[:, t * 128 : (t + 1) * 128]
-                    parts.append([fa[p, pl.ds(7 + k, 16, 2), :].astype(BF) for k in range(3)])
-                for a, i in uses(p, 2):
-                    for k in range(3):
-                        h, l = slot(9 * i + 3 * j + k)
-                        for t in range(2):
-                            im2[h, a, v, :, l * 256 + t * 128 : l * 256 + (t + 1) * 128] = parts[t][k]
-
-    loop(4, hidden_patches)
-
-    def second_filters(half, dst, kind):
-        lhs = cott[0].reshape(256, 128)
-
-        def body(n):
-            at = pl.ds(pl.multiple_of(n * 512, 512), 512)
-            dst[:, at] = dot(lhs, im2[half, :, :, :, at].reshape(128, 512)).astype(kind)
-
-        loop(7, body)
-
-    def first_filters(half, dst, kind):
-        lhs = jnp.concatenate([pbt[q, p] for q in range(2) for p in range(4)], axis=1)
-
-        def body(n):
-            at = pl.ds(pl.multiple_of(n * 256, 256), 256)
-            dst[:, at] = dot(lhs, im1[half, :, :, :, :, at].reshape(1024, 256)).astype(kind)
-
-        loop(7, body)
-
-    class Sum:
-        def __init__(self, refs, e):
-            self.e = e
-            (self.own, self.out, self.other, self.chip, self.yr, self.ys, self.fin) = refs[:7]
-            self.recv = refs[7:10], refs[10:13], refs[13:16]
-            self.yq, self.yp, self.full = refs[16:19]
-            w = [e, 5 * e, 5 * e]
-            self.width = w
-            self.begin = [0, 4 * e, 9 * e]
-            self.order = "zx", "zx", "xz"
-
-        def pair(self, filters):
-            filters(1 - core, self.out, BF)
-            self.link = put(self.out, self.other, sib)
-
-        def start(self):
-            arrived([self.link])
-
-            def body(n):
-                at = pl.ds(pl.multiple_of(n * 16, 16), 16)
-                total = self.own[at] + self.other[at].astype(F32)
-                self.chip[lax.div(n, 4), lax.rem(n, 4)] = total.astype(BF)
-
-            loop(16, body)
-            e = self.e
-            self.copies = []
-            for o in (1, 2, 3):
-                to = lax.rem(y + o, 4)
-                at = pl.ds(pl.multiple_of(to * e, e), e)
-                self.copies.append(put(self.chip.at[:, :, :, at], self.yr.at[o - 1], {"y": to}))
-            self.first = [None, self.send_first(1), self.send_first(2)]
-
-        def source(self, part):
-            if part == 0:
-                return self.ys, pl.ds(0, self.e)
-            return self.chip, pl.ds(self.begin[part], self.width[part])
-
-        def send_first(self, part):
-            src, at = self.source(part)
-            name, me = ("z", z) if self.order[part][0] == "z" else ("x", x)
-            out = []
-            for o in (1, 2, 3):
-                to = lax.rem(me + o, 4)
-                view = src.at[to, :, :, at] if name == "z" else src.at[:, to, :, at]
-                out.append(put(view, self.recv[part][0].at[o - 1], {name: to}))
-            return out
-
-        def shared(self):
-            arrived(self.copies)
-            e = self.e
-            at = pl.ds(pl.multiple_of(y * e, e), e)
-
-            def body(n):
-                total = self.chip[n, :, :, at].astype(F32)
-                for o in range(3):
-                    total += self.yr[o, n].astype(F32)
-                self.ys[n] = total.astype(BF)
-
-            loop(4, body)
-            self.first[0] = self.send_first(0)
-
-        def second(self, part):
-            arrived(self.first[part])
-            src, at = self.source(part)
-            got, mid, _ = self.recv[part]
-            total = (src[z, :, :, at] if self.order[part][0] == "z" else src[:, x, :, at]).astype(F32)
-            for o in range(3):
-                total += got[o].astype(F32)
-            mid[...] = total.astype(BF)
-            name, me = ("x", x) if self.order[part][0] == "z" else ("z", z)
-            out = []
-            for o in (1, 2, 3):
-                to = lax.rem(me + o, 4)
-                out.append(put(mid.at[to], self.recv[part][2].at[o - 1], {name: to}))
-            self.first[part] = out
-
-        def third(self, part):
-            arrived(self.first[part])
-            _, mid, got = self.recv[part]
-            total = (mid[x] if self.order[part][0] == "z" else mid[z]).astype(F32)
-            for o in range(3):
-                total += got[o].astype(F32)
-            e = self.e
-            if part == 0:
-                self.fin[y] = total.astype(BF)
-                self.last0 = [put(self.fin.at[y], self.fin.at[y], along("y", y, o)) for o in (1, 2, 3)]
-            else:
-                at = slice((part - 1) * 5 * e, part * 5 * e)
-                self.yq[:, at] = total.astype(BF)
-
-        def fourth(self):
-            self.last1 = [put(self.yq, self.yp.at[o - 1], along("y", y, o)) for o in (1, 2, 3)]
-
-        def final(self):
-            e = self.e
-            arrived(self.last0)
-            for n in range(4):
-                self.full[core, :, n * e : (n + 1) * e] = self.fin[n].astype(F32)
-            arrived(self.last1)
-            total = self.yq[...].astype(F32)
-            for o in range(3):
-                total += self.yp[o].astype(F32)
-            self.full[core, :, 4 * e : 14 * e] = total
-            self.done = put(self.full.at[core], self.full.at[core], sib)
-
-    sum1, sum2 = Sum(sums1, 128), Sum(sums2, 256)
-    sum2.pair(second_filters)
-    second_filters(core, sum2.own, F32)
     sum1.pair(first_filters)
-    sum2.start()
     first_filters(core, sum1.own, F32)
     sum1.start()
 
-    total = jnp.zeros((256, 128), F32)
-    for h in range(2):
-        total += dot_nt(wf2[h].reshape(256, 3584), im2[h].reshape(128, 3584))
-    ot[...] = total.astype(BF).reshape(16, 16, 128)
+    for row in range(2):
+        total = jnp.zeros((256, 128), F32)
+        for tap in range(27):
+            if (tap // 3 % 3 == 0) == (row == 1):
+                h, l = slot(tap)
+                at = slice(l * 256, (l + 1) * 256)
+                total += dot_nt(wf2[h, :, :, :, at].reshape(256, 256), im2[h, :, :, :, at].reshape(128, 256))
+        ot[:, row] = total.astype(BF).reshape(16, 16, 128)
     outs = []
     for o in range(1, 16):
         dev = chan_at(o)
-        outs.append(put(ot.at[dev["z"] * 4 + dev["x"]], so.at[chan], dev))
-    so[chan] = ot[chan]
-    sum2.shared()
-
-    arrived(pb_halo)
-
-    @pl.when(chan == 15)
-    def _():
-        pb0[2] = jnp.zeros((5, 4, 32, 256), BF)
+        outs.append(put(ot.at[dev["z"] * 4 + dev["x"]], sor.at[chan], dev))
+    sor[chan] = ot[chan]
+    arrived(pb_halo[1:2])
 
     @pl.when(space == 7)
     def _():
-        pb0[:, 4] = jnp.zeros((3, 4, 32, 256), BF)
+        pb0[0:2, 4] = jnp.zeros((2, 4, 32, 256), BF)
 
     edge = lax.broadcasted_iota(jnp.int32, (128, 256), 0) % 32 == 31
 
@@ -506,7 +508,7 @@
             rows = jnp.where(edge, 0.0, pltpu.roll(rows, 127, 0))
             pb1[q, p] = rows.astype(BF).reshape(4, 32, 256)
 
-    loop(3, shifted)
+    loop(2, shifted)
 
     def volume_grad(q):
         def body(n):
@@ -537,24 +539,39 @@
         loop(2, body)
 
     volume_grad(0)
-    sum1.shared()
+    sum2.shared()
     sum2.second(1)
     sum2.second(2)
+    sum1.shared()
     sum2.second(0)
-    volume_grad(1)
     sum1.second(1)
     sum1.second(2)
-    sum1.second(0)
     for part in (1, 2):
         sum2.third(part)
     sum2.fourth()
+    sum1.second(0)
     sum2.third(0)
+    arrived(pb_halo[0:1] + pb_halo[2:3])
+
+    @pl.when(chan == 15)
+    def _():
+        pb0[2] = jnp.zeros((5, 4, 32, 256), BF)
+
+    @pl.when(space == 7)
+    def _():
+        pb0[2, 4] = jnp.zeros((4, 32, 256), BF)
+
+    shifted(2)
     for part in (1, 2):
         sum1.third(part)
     sum1.fourth()
     sum1.third(0)
+    volume_grad(1)
+    sum2.final()
     arrived(outs)
-    sum2.final()
+    so[0] = sor[0, 0]
+    for b in range(1, 16):
+        so[b] = (sor[b, 0].astype(F32) + sor[b - 1, 1].astype(F32)).astype(BF)
     sum1.final()
     arrived([sum2.done])
     for h in range(2):
@@ -639,7 +656,7 @@
             pltpu.VMEM((2, 16, 3584), BF),
             pltpu.VMEM((2, 4, 4, 32, 256), F32),
             pltpu.VMEM((2, 4, 4, 2, 32, 128), F32),
-            pltpu.VMEM((3, 5, 4, 32, 256), BF),
+            pltpu.VMEM((2, 5, 4, 32, 256), BF),
             pltpu.VMEM((3, 5, 4, 32, 256), BF),
             pltpu.VMEM((3, 5, 4, 32, 256), BF),
             pltpu.VMEM((2, 4, 256, 128), BF),
@@ -652,7 +669,8 @@
             pltpu.VMEM((8, 64, 128), F32),
             *sums(128),
             *sums(256),
-            pltpu.VMEM((16, 16, 128), BF),
+            pltpu.VMEM((16, 2, 16, 128), BF),
+            pltpu.VMEM((16, 2, 16, 128), BF),
             pltpu.VMEM((2, 8, 64, 128), BF),
             pltpu.SemaphoreType.DMA((NSEM,)),
             pltpu.SemaphoreType.DMA((NSEM,)),

time: 87.8 us -> 86.7 us (0.987)
  Pallas kernels: 87 us -> 85.9 us
    pallas_call x1, Pallas kernels: 82.4 us -> 81.3 us  [local(): pl.pallas_call(kernel, out_shape=(jax.ShapeDtypeStruct((16, 16, 128), BF)...]
where the time goes in v3:
time: 86.7 us; the launch traced here: 86.5 us
  Pallas kernels  85.9 us (99%)
    pallas_call x1, Pallas kernels, local(): pl.pallas_call(kernel, out_shape=(jax.ShapeDtypeStruct((16, 16, 128), BF)...  81.3 us
    pallas_call x1, Pallas kernels, local(): pl.pallas_call(finish, out_shape=(jax.ShapeDtypeStruct((4, 2, 16, 16, 16)...  4.6 us

profile of v3, /device:TPU:1, one launch (start us, length us, event | category | flops | bytes accessed | tf_op | source)
XLA Modules:
  0.0 86.5 jit_solution(12161546935459905272)
XLA Ops:
  0.6 81.3 %two_layers.1 = (bf16[16,16,128]{2,1,0:T(8,128)(2,1)}, bf16[4,8,4,64,128]{4,3,2,1,0:T(8,128)(2,1)}, f32[2,16,1792]{2,1,0:T(8,128)}, f32[2,16,3584]{2,1,0:T(8,128)}) custom-call(bf16[4,8,4,64,128]{4,3,2,1,0:T(8,128)(2,1)} %vol.1, bf16[27,16,128]{2,1,0:T(8,128)(2,1)} %bitcast.15, bf16[27,16,256]{2,1,0:T(8,128)(2,1)} %bitcast.13, bf16[4,2,16,16,16]{4,3,2,1,0:T(8,128)(2,1)} %cot.1), custom_call_target="tpu_custom_call" | custom-call | flops 6800000000 | bytes 6000000 | tf_op jit(solution)/shard_map/two_layers/pallas_call | solution.py:639
  81.9 4.6 %finish.1 = (bf16[4,2,16,16,16]{4,3,2,1,0:T(8,128)(2,1)}, bf16[4,8,4,64,128]{4,3,2,1,0:T(8,128)(2,1)}, f32[27,16,128]{2,1,0:T(8,128)}, f32[27,16,256]{2,1,0:T(8,128)}) custom-call(bf16[16,16,128]{2,1,0:T(8,128)(2,1)} %get-tuple-element.12.so, bf16[4,8,4,64,128]{4,3,2,1,0:T(8,128)(2,1)} %get-tuple-element.13.vg, f32[2,16,1792]{2,1,0:T(8,128)} %get-tuple-element.14.g1, ...), custom_call_target="tpu_custom_call" | custom-call | tf_op jit(solution)/shard_map/finish/pallas_call | solution.py:687

commit v4 on v3

--- a/solution.py
+++ b/solution.py
@@ -51,7 +51,7 @@
     *rest,
 ):
     sums1, sums2 = rest[:NSUM], rest[NSUM : 2 * NSUM]
-    ot, sor, relay, ssem, rsem, lsem, hsend, hrecv = rest[2 * NSUM :]
+    ot, sor, vgv, relay, ssem, rsem, lsem, hsend, hrecv = rest[2 * NSUM :]
     y, core = lax.axis_index("y"), lax.axis_index("core")
     z, x = lax.axis_index("z"), lax.axis_index("x")
     chan = z * 4 + x
@@ -150,7 +150,7 @@
         part = full.at[core, :, :, :, at]
         return put(part, part, sib)
 
-    (p1, q1, r1), (p2, q2, r2) = cut(128, 4, 6), cut(256, 4, 6)
+    (p1, q1, r1), (p2, q2, r2) = cut(128, 4, 5), cut(256, 4, 5)
     w1_px, w1_qx, w1_rz = one_row(w1o, wf1, p1, "x"), one_row(w1o, wf1, q1, "x"), one_row(w1o, wf1, r1, "z")
     w2_px, w2_rz, w2_qx = one_row(w2o, wf2, p2, "x"), one_row(w2o, wf2, r2, "z"), one_row(w2o, wf2, q2, "x")
     vol_plane = put(vol.at[:, 7], xv.at[:, 0, 1:5], space_at(1))
@@ -534,11 +534,13 @@
                             m = (p * 4 + v) * 32
                             vs[p * 4 + v, pl.ds(0, 32, 2), :] = total[m : m + 32, 0:128]
                             vs[p * 4 + v, pl.ds(1, 32, 2), :] = extra[m : m + 32]
-                            vg[v, 4 * n + 2 * p + s1, 2 * q + s2] = vs[p * 4 + v].astype(BF)
+                            vgv[v, 4 * n + 2 * p + s1, 2 * q + s2] = vs[p * 4 + v].astype(BF)
 
         loop(2, body)
 
     volume_grad(0)
+    grads = [pltpu.make_async_copy(vgv.at[:, :, 0:2], vg.at[:, :, 0:2], lsem.at[0])]
+    grads[0].start()
     sum2.shared()
     sum2.second(1)
     sum2.second(2)
@@ -567,6 +569,8 @@
     sum1.fourth()
     sum1.third(0)
     volume_grad(1)
+    grads.append(pltpu.make_async_copy(vgv.at[:, :, 2:4], vg.at[:, :, 2:4], lsem.at[1]))
+    grads[1].start()
     sum2.final()
     arrived(outs)
     so[0] = sor[0, 0]
@@ -579,6 +583,8 @@
     arrived([sum1.done])
     for h in range(2):
         g1[h] = sum1.full[h]
+    for copy in grads:
+        copy.wait()
     for copy in sent:
         copy.wait_send()
     vol_half.copy.wait_send()
@@ -645,7 +651,7 @@
             jax.ShapeDtypeStruct((2, 16, 3584), F32),
         ),
         in_specs=[anywhere, vmem, vmem, anywhere],
-        out_specs=(vmem, vmem, vmem, vmem),
+        out_specs=(vmem, anywhere, vmem, vmem),
         scratch_shapes=[
             pltpu.VMEM((4, 9, 5, 64, 128), BF),
             pltpu.VMEM((2, 2, 4, 4, 32, 1792), BF),
@@ -671,6 +677,7 @@
             *sums(256),
             pltpu.VMEM((16, 2, 16, 128), BF),
             pltpu.VMEM((16, 2, 16, 128), BF),
+            pltpu.VMEM((4, 8, 4, 64, 128), BF),
             pltpu.VMEM((2, 8, 64, 128), BF),
             pltpu.SemaphoreType.DMA((NSEM,)),
             pltpu.SemaphoreType.DMA((NSEM,)),

time: 86.7 us -> 85.8 us (0.990)
  Pallas kernels: 85.9 us -> 85 us
    pallas_call x1, Pallas kernels: 81.3 us -> 80.4 us  [local(): pl.pallas_call(kernel, out_shape=(jax.ShapeDtypeStruct((16, 16, 128), BF)...]
where the time goes in v4:
time: 85.8 us; the launch traced here: 85.6 us
  Pallas kernels  85 us (99%)
    pallas_call x1, Pallas kernels, local(): pl.pallas_call(kernel, out_shape=(jax.ShapeDtypeStruct((16, 16, 128), BF)...  80.4 us
    pallas_call x1, Pallas kernels, local(): pl.pallas_call(finish, out_shape=(jax.ShapeDtypeStruct((4, 2, 16, 16, 16)...  4.6 us

profile of v4, /device:TPU:1, one launch (start us, length us, event | category | flops | bytes accessed | tf_op | source)
XLA Modules:
  0.0 85.6 jit_solution(7819874685162122502)
XLA Ops:
  0.6 80.4 %two_layers.1 = (bf16[16,16,128]{2,1,0:T(8,128)(2,1)}, bf16[4,8,4,64,128]{4,3,2,1,0:T(8,128)(2,1)}, f32[2,16,1792]{2,1,0:T(8,128)}, f32[2,16,3584]{2,1,0:T(8,128)}) custom-call(bf16[4,8,4,64,128]{4,3,2,1,0:T(8,128)(2,1)} %vol.1, bf16[27,16,128]{2,1,0:T(8,128)(2,1)} %bitcast.15, bf16[27,16,256]{2,1,0:T(8,128)(2,1)} %bitcast.13, bf16[4,2,16,16,16]{4,3,2,1,0:T(8,128)(2,1)} %cot.1), custom_call_target="tpu_custom_call" | custom-call | flops 6800000000 | bytes 6000000 | tf_op jit(solution)/shard_map/two_layers/pallas_call | solution.py:645
  81.0 4.6 %finish.1 = (bf16[4,2,16,16,16]{4,3,2,1,0:T(8,128)(2,1)}, bf16[4,8,4,64,128]{4,3,2,1,0:T(8,128)(2,1)}, f32[27,16,128]{2,1,0:T(8,128)}, f32[27,16,256]{2,1,0:T(8,128)}) custom-call(bf16[16,16,128]{2,1,0:T(8,128)(2,1)} %get-tuple-element.12.so, bf16[4,8,4,64,128]{4,3,2,1,0:T(8,128)(2,1)} %get-tuple-element.13.vg, f32[2,16,1792]{2,1,0:T(8,128)} %get-tuple-element.14.g1, ...), custom_call_target="tpu_custom_call" | custom-call | tf_op jit(solution)/shard_map/finish/pallas_call | solution.py:694
